TPU v7x, 128 devices: a whole 4x4x4 slice. The times are simulated.
128 devices in a mesh: row: 16 (over z_hi, y, core), col: 8 (over x, z_lo).
Axes of the slice: x: 4, y: 4, z: 4 (z_hi: 2, z_lo: 2; z = z_hi * 2 + z_lo), core: 2. Of those that a mesh axis runs over, the one named last changes fastest.
Arguments:
- operator: bfloat16 [36864, 36864], P('row', 'col'), may hold values from -0.046875 to 0.046875
- sketch_right: bfloat16 [36864, 384], P(('col', 'row')), may hold values from -6 to 6
- sketch_left: bfloat16 [36864, 576], P(('row', 'col')), may hold values from -6 to 6
Outputs:
- left_factor: bfloat16 [36864, 384], P('row')
- right_factor: bfloat16 [36864, 384], P(('col', 'row'))
All inputs are finite; a program needn't handle non-finite values.
Results may differ from a plain program's by a relative error of at most 0.0015.
Values may be sent and summed in bfloat16 or wider, within the bound.
No kernel may reach another device: no remote copies, remote signals or barrier semaphores. Data moves between devices by JAX's collectives and lax.ppermute only.
A program may use at most 128 MiB of HBM per device.

v0:
```python
import math

import jax
import jax.numpy as jnp
from jax import lax
from jax.sharding import PartitionSpec as P

N = 36864
L = 576


def transposed_product(wide, sketch):
    contract = (((0,), (0,)), ((), ()))
    high_part = wide.astype(jnp.bfloat16)
    rest = wide - lax.optimization_barrier(high_part).astype(jnp.float32)
    middle_part = rest.astype(jnp.bfloat16)
    low_part = (rest - lax.optimization_barrier(middle_part).astype(jnp.float32)).astype(
        jnp.bfloat16
    )
    total = lax.dot_general(high_part, sketch, contract, preferred_element_type=jnp.float32)
    total = total + lax.dot_general(
        middle_part, sketch, contract, preferred_element_type=jnp.float32
    )
    return total + lax.dot_general(low_part, sketch, contract, preferred_element_type=jnp.float32)


def on_device(operator, sketch_right, sketch_left):
    right_rows = lax.all_gather(sketch_right, "row", axis=0, tiled=True)
    left_rows = lax.all_gather(sketch_left, "col", axis=0, tiled=True)
    contract = (((0,), (0,)), ((), ()))
    wide_piece = lax.psum_scatter(
        lax.dot_general(operator, left_rows, contract, preferred_element_type=jnp.float32),
        "row",
        scatter_dimension=0,
        tiled=True,
    )
    core_term = transposed_product(wide_piece, sketch_right)
    core = lax.psum(core_term, ("row", "col"))
    gram = jnp.dot(core.T, core, precision=lax.Precision.HIGHEST)
    lower = jnp.linalg.cholesky(gram)
    identity = jnp.eye(gram.shape[0], dtype=jnp.float32)
    inverse = jax.scipy.linalg.solve_triangular(lower, identity, lower=True).T
    ortho = jnp.dot(core, inverse, precision=lax.Precision.HIGHEST)
    right_factor = jnp.dot(wide_piece, ortho, precision=lax.Precision.HIGHEST).astype(jnp.bfloat16)
    factor = math.sqrt(N * L)
    image_term = jnp.dot(operator, right_rows, preferred_element_type=jnp.float32)
    image_rows = lax.psum(image_term, "col")
    left_factor = (factor * jnp.dot(image_rows, inverse, precision=lax.Precision.HIGHEST)).astype(
        jnp.bfloat16
    )
    return (left_factor, right_factor)


def solution(mesh):
    in_specs = (P("row", "col"), P(("col", "row"), None), P(("row", "col"), None))
    out_specs = (P("row", None), P(("col", "row"), None))
    return jax.shard_map(
        on_device, mesh=mesh, in_specs=in_specs, out_specs=out_specs, check_vma=False
    )
```

profile of v0, /device:TPU:1, one launch (start us, length us, event | category | flops | bytes accessed | tf_op | source)
XLA Modules:
  0.0 602.1 jit_solution(14986135669976520425)
XLA Ops:
  7.2 0.7 all-gather.5.cloned.1.call-update
  7.9 71.1 %all-gather.5.cloned.1.call-done = bf16[2304,576]{1,0:T(8,128)(2,1)} async-done(((bf16[288,576]{1,0:T(8,128)(2,1)}), bf16[2304,576]{1,0:T(8,128)(2,1)}) %all-gather.5.cloned.1.call-update) | async-done | bytes 2654224 | tf_op jit(solution)/shard_map/all_gather | solution.py:29
  79.0 22.6 %fusion.26 = f32[4608,576]{1,0:T(8,128)} fusion(bf16[2304,4608]{1,0:T(8,128)(2,1)} %param.3, bf16[2304,576]{1,0:T(8,128)(2,1)} %all-gather.5.cloned.1.call-done), kind=kOutput, calls=%fused_computation.61 | convolution fusion | flops 12230590464 | bytes 34504704 | tf_op jit(solution)/shard_map/dot_general | solution.py:32
  101.7 0.7 all-gather.3.cloned.1.call-update
  102.5 0.7 iota_compare_fusion
  103.2 118.0 %reduce-scatter.2.cloned.1.call-done = f32[288,576]{1,0:T(8,128)} async-done(((f32[4608,576]{1,0:T(8,128)}), f32[288,576]{1,0:T(8,128)}) %reduce-scatter.2.cloned.1.call-update) | async-done | bytes 663568 | tf_op jit(solution)/shard_map/reduce_scatter | solution.py:31
  221.2 1.2 convert_element_type.26
  222.4 1.2 fusion.2
  224.6 1.4 convolution_add_fusion
  226.1 51.0 %all-gather.3.cloned.1.call-done = bf16[4608,384]{1,0:T(8,128)(2,1)} async-done(((bf16[288,384]{1,0:T(8,128)(2,1)}), bf16[4608,384]{1,0:T(8,128)(2,1)}) %all-gather.3.cloned.1.call-update) | async-done | bytes 3538960 | tf_op jit(solution)/shard_map/all_gather | solution.py:28
  277.1 18.0 %fusion.25 = f32[2304,384]{1,0:T(8,128)} fusion(bf16[2304,4608]{1,0:T(8,128)(2,1)} %param.3, bf16[4608,384]{1,0:T(8,128)(2,1)} %all-gather.3.cloned.1.call-done), kind=kOutput, calls=%fused_computation.60 | convolution fusion | flops 8153726976 | bytes 28311552 | tf_op jit(solution)/shard_map/dot_general | solution.py:46
  295.2 132.6 %all-reduce.6.cloned.1.call-done = f32[576,384]{1,0:T(8,128)} async-done(((f32[576,384]{1,0:T(8,128)}), f32[576,384]{1,0:T(8,128)}) %all-reduce.6.cloned.1.call-update) | async-done | bytes 884752 | tf_op jit(solution)/shard_map/psum | solution.py:38
  427.8 3.5 fusion.28
  431.6 11.7 %cholesky.77 = f32[128,128]{1,0:T(8,128)S(1)} custom-call(f32[128,128]{1,0:T(8,128)S(1)} %cholesky.192), custom_call_target="Cholesky" | custom-call | tf_op jit(solution)/shard_map/jit(cholesky)/cholesky | solution.py:40
  443.4 9.8 %custom-call.23 = f32[1,128,128]{1,2,0:T(8,128)S(1)} custom-call(f32[1,128,128]{2,1,0:T(8,128)S(1)} %get-tuple-element.26), custom_call_target="InvertDiagBlocksLowerTriangular" | custom-call | tf_op jit(solution)/shard_map/jit(cholesky)/cholesky | solution.py:40
  454.4 13.3 %cholesky.162 = f32[128,128]{1,0:T(8,128)} custom-call(f32[128,128]{1,0:T(8,128)} %cholesky.196), custom_call_target="Cholesky" | custom-call | tf_op jit(solution)/shard_map/jit(cholesky)/cholesky | solution.py:40
  467.8 1.5 select_reduce_fusion.1
  469.2 11.3 %custom-call.24 = f32[1,128,128]{1,2,0:T(8,128)} custom-call(f32[1,128,128]{2,1,0:T(8,128)} %get-tuple-element.23), custom_call_target="InvertDiagBlocksLowerTriangular" | custom-call | tf_op jit(solution)/shard_map/jit(cholesky)/cholesky | solution.py:40
  480.5 1.0 convolution_dynamic-update-slice_fusion
  481.8 11.7 %cholesky.181 = f32[128,128]{1,0:T(8,128)S(1)} custom-call(f32[128,128]{1,0:T(8,128)S(1)} %convolution_subtract_fusion.3), custom_call_target="Cholesky" | custom-call | tf_op jit(solution)/shard_map/jit(cholesky)/cholesky | solution.py:40
  493.6 0.7 compare_reduce_fusion.1
  495.7 0.6 compare_reduce_fusion
  497.0 8.2 %while.1 = (s32[]{:T(128)}, f32[384,384]{1,0:T(8,128)S(1)}, s32[3,2]{0,1:T(2,128)S(1)}, f32[3,128,128]{2,1,0:T(8,128)}, s32[]{:T(128)}) while((s32[]{:T(128)}, f32[384,384]{1,0:T(8,128)S(1)}, s32[3,2]{0,1:T(2,128)S(1)}, f32[3,128,128]{2,1,0:T(8,128)}, s32[]{:T(128)}) %tuple.29), condition=%wide.while_cond, body=%wide.while_body.sunk | while | flops 2 | bytes 132705 | solution.py:42
  497.7 2.1 bitcast_dynamic-update-slice_fusion.2
  500.4 2.1 bitcast_dynamic-update-slice_fusion.2
  503.2 2.1 bitcast_dynamic-update-slice_fusion.2
  505.2 30.5 %custom-call.25 = f32[3,128,128]{1,2,0:T(8,128)S(1)} custom-call(f32[3,128,128]{2,1,0:T(8,128)} %get-tuple-element.9), custom_call_target="InvertDiagBlocksLowerTriangular" | custom-call | tf_op jit(solution)/shard_map/jit(_solve_triangular)/triangular_solve | solution.py:42
  535.7 1.0 fusion.7
  538.3 1.8 fusion.3
  540.1 2.2 convolution_convert_fusion
  542.2 43.9 %all-reduce.4.cloned.1.call-done = f32[2304,384]{1,0:T(8,128)} async-done(((f32[2304,384]{1,0:T(8,128)}), f32[2304,384]{1,0:T(8,128)}) %all-reduce.4.cloned.1.call-update) | async-done | bytes 3538960 | tf_op jit(solution)/shard_map/psum | solution.py:47
  586.1 9.2 %fusion = bf16[2304,384]{1,0:T(8,128)(2,1)} fusion(f32[2304,384]{1,0:T(8,128)} %all-reduce.4.cloned.1.call-done, f32[128,384]{1,0:T(8,128)S(1)} %fusion.14, f32[128,384]{1,0:T(8,128)S(1)} %fusion.16, f32[128,384]{1,0:T(8,128)S(1)} %fusion.7), kind=kOutput, calls=%fused_computation.3 | convolution fusion | flops 4078927872 | bytes 5898240 | tf_op jit(solution)/shard_map/dot_general | solution.py:48
  (41 shorter events, 6.6 us)
Async XLA Ops:
  7.2 71.9 %all-gather.5.cloned.1.call-start = ((), (), s32[]{:S(2)}) async-start(), calls=%async_computation.3 | async-start | bytes 3317760 | tf_op jit(solution)/shard_map/all_gather | solution.py:29
  7.9 213.3 %reduce-scatter.2.cloned.1.call-start = ((), (), s32[]{:S(2)}) async-start(), calls=%async_computation.4 | async-start | bytes 12533760 | tf_op jit(solution)/shard_map/reduce_scatter | solution.py:31
  101.7 122.0 %copy-start.2 = (bf16[288,384]{1,0:T(8,128)(2,1)S(1)}, bf16[288,384]{1,0:T(8,128)(2,1)}, u32[]{:S(2)}) copy-start(bf16[288,384]{1,0:T(8,128)(2,1)} %param.4) | copy-start | bytes 663556
  101.7 175.5 %all-gather.3.cloned.1.call-start = ((), (), s32[]{:S(2)}) async-start(), calls=%async_computation.1 | async-start | bytes 3760128 | tf_op jit(solution)/shard_map/all_gather | solution.py:28
  102.4 325.4 %all-reduce.6.cloned.1.call-start = ((), (), s32[]{:S(2)}) async-start(), calls=%async_computation.5 | async-start | bytes 1769472 | tf_op jit(solution)/shard_map/psum | solution.py:38
  221.2 3.4 copy-start
  226.1 360.1 %all-reduce.4.cloned.1.call-start = ((), (), s32[]{:S(2)}) async-start(), calls=%async_computation.2 | async-start | bytes 7077888 | tf_op jit(solution)/shard_map/psum | solution.py:47
  453.2 85.1 %copy-start.1 = (f32[576,384]{1,0:T(8,128)S(1)}, f32[576,384]{1,0:T(8,128)}, u32[]{:S(2)}) copy-start(f32[576,384]{1,0:T(8,128)} %all-reduce.6.cloned.1.call-done) | copy-start | bytes 2654212
Sparse Core Ops, SparseCore 0:
  9.6 69.3 all-gather.4
  101.8 119.3 reduce-scatter.1
  223.9 53.1 all-gather.2
  283.1 144.6 all-reduce.5
  430.2 155.9 all-reduce.3
where the time goes:
time: 609 us; the launch traced here: 602 us
  waiting for transfers between devices  418 us (69%)
  other arithmetic  94.5 us (16%)
  matrix products  64 us (11%)
  between operations  16.2 us (3%)
  local copies, waits for them, and re-layouts  9.12 us (1%)
    psum x1, waiting for transfers between devices, on_device(): core = lax.psum(core_term, ('row', 'col'))  133 us
    reduce_scatter x1, waiting for transfers between devices, on_device(): lax.psum_scatter(lax.dot_general(operator, left_rows, contract, preferred...  118 us
    all_gather x1, waiting for transfers between devices, on_device(): left_rows = lax.all_gather(sketch_left, 'col', axis=0, tiled=True)  71.1 us
    another operation x10, other arithmetic, on_device(): lower = jnp.linalg.cholesky(gram)  60.7 us
    all_gather x1, waiting for transfers between devices, on_device(): right_rows = lax.all_gather(sketch_right, 'row', axis=0, tiled=True)  51 us
    psum x1, waiting for transfers between devices, on_device(): image_rows = lax.psum(image_term, 'col')  43.9 us
    another operation x3, other arithmetic, on_device(): inverse = jax.scipy.linalg.solve_triangular(lower, identity, lower=True).T  30.6 us
    dot_general x1, matrix products, on_device(): lax.dot_general(operator, left_rows, contract, preferred_element_type=jnp...  22.6 us
  transfers between devices with their start and end apart: 5, of which 5 were waited for; matrix products, arithmetic and copies ran while one was open for 23% of the time, Pallas kernels for 0%

commit v1 on v0

v1 whole, which is shorter than its diff:
```python
import functools
import math

import jax
import jax.numpy as jnp
from jax import lax
from jax.experimental import pallas as pl
from jax.experimental.pallas import tpu as pltpu
from jax.sharding import PartitionSpec as P

N = 36864
L = 576
BLOCK = 128
PANEL = 16
HIGHEST = lax.Precision.HIGHEST
TRANSPOSED = (((0,), (0,)), ((), ()))
CORE, ROW_RING, ROW_Z = 1, (2, 6, 4), 8
COL_RING, COL_Z = (2, 6, 4), 1


def three_parts(value):
    high_part = value.astype(jnp.bfloat16)
    rest = value - lax.optimization_barrier(high_part).astype(jnp.float32)
    middle_part = rest.astype(jnp.bfloat16)
    low_part = (rest - lax.optimization_barrier(middle_part).astype(jnp.float32)).astype(
        jnp.bfloat16
    )
    return high_part, middle_part, low_part


def kernel_parts(value):
    high = value.astype(jnp.bfloat16).astype(jnp.float32)
    rest = value - high
    middle = rest.astype(jnp.bfloat16).astype(jnp.float32)
    low = (rest - middle).astype(jnp.bfloat16).astype(jnp.float32)
    return high, middle, low


def rank_update(value):
    high, middle, low = kernel_parts(value)
    left = jnp.concatenate([high, high, middle, high, low, middle], 0).astype(jnp.bfloat16)
    right = jnp.concatenate([high, middle, high, low, high, middle], 0).astype(jnp.bfloat16)
    return lax.dot_general(left, right, TRANSPOSED, preferred_element_type=jnp.float32)


def block_factor(block_ref):
    size = block_ref.shape[0]
    row = lax.broadcasted_iota(jnp.int32, (PANEL, size), 0)
    lane = lax.broadcasted_iota(jnp.int32, (PANEL, size), 1)
    for start in range(0, size, PANEL):
        end = start + PANEL
        panel = block_ref[start:end, :]
        rows = jnp.where(
            (lane >= start) & (lane < end), (lane - start == row).astype(jnp.float32), panel
        )
        columns = [
            jnp.broadcast_to(panel[:, start + j : start + j + 1], (PANEL, size))
            for j in range(PANEL)
        ]
        pivots = jnp.ones((PANEL, size), jnp.float32)
        for i in range(PANEL):
            pivot = columns[i][i : i + 1, :]
            multiple = jnp.where(row > i, columns[i] * (1.0 / pivot), 0.0)
            pivots = jnp.where(row == i, pivot, pivots)
            for j in range(i + 1, PANEL):
                columns[j] = columns[j] - multiple * columns[j][i : i + 1, :]
            rows = rows - multiple * rows[i : i + 1, :]
        rows = rows * lax.rsqrt(pivots)
        block_ref[start:end, :] = rows
        if end < size:
            below = lax.broadcasted_iota(jnp.int32, (size - end, size), 1)
            rest = jnp.where((below >= start) & (below < end), 0.0, block_ref[end:, :])
            block_ref[end:, :] = rest - rank_update(rows)[end:, :]
    down = lax.broadcasted_iota(jnp.int32, (size, size), 0)
    across = lax.broadcasted_iota(jnp.int32, (size, size), 1)
    return jnp.where(down >= across, block_ref[...], 0.0)


def factor_kernel(core_ref, lower_inverse_ref, ortho_ref, block_ref):
    core = core_ref[...]
    size = core.shape[1]
    work = lower_inverse_ref
    dot = functools.partial(
        lax.dot_general, precision=HIGHEST, preferred_element_type=jnp.float32
    )
    work[...] = dot(core, core, TRANSPOSED)
    starts = range(0, size, BLOCK)
    for low in starts:
        high = low + BLOCK
        block_ref[...] = work[low:high, low:high]
        inverse = block_factor(block_ref)
        strip = dot(inverse, work[low:high, :], (((1,), (0,)), ((), ())))
        strip = jnp.concatenate(
            [inverse if at == low else strip[:, at : at + BLOCK] for at in starts], 1
        )
        if high < size:
            change = dot(strip[:, high:], strip, TRANSPOSED)
            for at in starts:
                old = 0.0 if at == low else work[high:, at : at + BLOCK]
                work[high:, at : at + BLOCK] = old - change[:, at : at + BLOCK]
        for at in starts:
            kept = strip[:, at : at + BLOCK]
            work[low:high, at : at + BLOCK] = kept if at <= low else jnp.zeros_like(kept)
    ortho_ref[...] = dot(core, work[...], (((1,), (1,)), ((), ())))


def factors_of(core):
    tall, size = core.shape
    return pl.pallas_call(
        factor_kernel,
        out_shape=[
            jax.ShapeDtypeStruct((size, size), jnp.float32),
            jax.ShapeDtypeStruct((tall, size), jnp.float32),
        ],
        scratch_shapes=[pltpu.VMEM((BLOCK, BLOCK), jnp.float32)],
        compiler_params=pltpu.CompilerParams(vmem_limit_bytes=32 * 2**20),
        cost_estimate=pl.CostEstimate(
            flops=20 * 10**9, bytes_accessed=3 * 10**6, transcendentals=0
        ),
    )(core)


def swap(value, axis, count, mask):
    return lax.ppermute(value, axis, [(i, i ^ mask) for i in range(count)])


def gather_direct(value, axes, count):
    copies = jnp.broadcast_to(value[None], (count,) + value.shape)
    return lax.all_to_all(copies, axes, 0, 0)


def sum_everywhere(value, count):
    pieces = value.reshape(count, -1)
    share = lax.all_to_all(pieces, ("row", "col"), 0, 0).sum(0)
    return gather_direct(share, ("row", "col"), count).reshape(value.shape)


def gather_grid(value, axis, count, ring, across, shift):
    me = lax.axis_index(axis)
    other = swap(value, axis, count, across)
    found = [(0, value)] + [(mask, swap(value, axis, count, mask)) for mask in ring]
    found += [(across, other)]
    found += [(across ^ mask, swap(other, axis, count, mask)) for mask in ring]
    whole = jnp.zeros((len(found),) + value.shape, value.dtype)
    for mask, shard in found:
        whole = lax.dynamic_update_index_in_dim(whole, shard, (me ^ mask) >> shift, 0)
    return whole


def on_device(rows, cols, operator, sketch_right, sketch_left):
    core_index = lax.axis_index("row") & 1
    own = gather_grid(sketch_right, "row", rows, ROW_RING, ROW_Z, 1)
    partner = swap(own, "row", rows, CORE)
    first = core_index == 0
    right_rows = jnp.stack(
        [jnp.where(first, own, partner), jnp.where(first, partner, own)], 1
    ).reshape(-1, sketch_right.shape[1])
    left_rows = gather_grid(sketch_left, "col", cols, COL_RING, COL_Z, 0)
    left_rows = left_rows.reshape(-1, sketch_left.shape[1])

    image_term = jnp.dot(operator, right_rows, preferred_element_type=jnp.float32)
    core_term = sum(
        lax.dot_general(left_rows, part, TRANSPOSED, preferred_element_type=jnp.float32)
        for part in three_parts(image_term)
    )
    image_piece = lax.all_to_all(
        image_term.reshape(cols, -1, image_term.shape[1]), "col", 0, 0
    ).sum(0)

    core_term, late_rows = lax.optimization_barrier((core_term, left_rows))
    wide_term = lax.dot_general(
        operator, late_rows, TRANSPOSED, preferred_element_type=jnp.float32
    )
    core = sum_everywhere(core_term, rows * cols)

    halves = wide_term.reshape(rows // 2, 2, -1, wide_term.shape[1])
    mine = lax.dynamic_index_in_dim(halves, core_index, 1, False)
    theirs = lax.dynamic_index_in_dim(halves, 1 - core_index, 1, False)
    paired = mine + swap(theirs, "row", rows, CORE)
    same_core = [[i for i in range(rows) if i % 2 == c] for c in range(2)]
    wide_piece = lax.all_to_all(paired, "row", 0, 0, axis_index_groups=same_core).sum(0)

    lower_inverse, ortho = factors_of(core)
    factor = math.sqrt(N * L)
    left_piece = (
        factor
        * lax.dot_general(
            image_piece,
            lower_inverse,
            (((1,), (1,)), ((), ())),
            precision=HIGHEST,
            preferred_element_type=jnp.float32,
        )
    ).astype(jnp.bfloat16)
    left_factor = gather_grid(left_piece, "col", cols, COL_RING, COL_Z, 0)
    left_factor = left_factor.reshape(-1, left_piece.shape[1])
    right_factor = jnp.dot(wide_piece, ortho, precision=HIGHEST).astype(jnp.bfloat16)
    return (left_factor, right_factor)


def solution(mesh):
    rows, cols = mesh.shape["row"], mesh.shape["col"]
    in_specs = (P("row", "col"), P(("col", "row"), None), P(("row", "col"), None))
    out_specs = (P("row", None), P(("col", "row"), None))
    return jax.shard_map(
        functools.partial(on_device, rows, cols),
        mesh=mesh,
        in_specs=in_specs,
        out_specs=out_specs,
        check_vma=False,
    )
```

time: 609 us -> 346 us (0.57)
  waiting for transfers between devices: 418 us -> 126 us
  other arithmetic: 94.5 us -> 22.2 us
  starting transfers between devices: 0.2 us -> 51.2 us
  local copies, waits for them, and re-layouts: 9.12 us -> 48.5 us
  blocking collectives: 0 us -> 22.9 us
  Pallas kernels: 0 us -> 15.8 us
  between operations: 16.2 us -> 1.06 us
  matrix products: 64 us -> 51.9 us
    psum x2 -> x0, waiting for transfers between devices: 176 us -> none  [the longest x1 133 us: on_device(): core = lax.psum(core_term, ('row', 'col'))]
    all_gather x2 -> x0, waiting for transfers between devices: 122 us -> none  [the longest x1 71.1 us: on_device(): left_rows = lax.all_gather(sketch_left, 'col', axis=0, tiled=True)]
    reduce_scatter x1 -> x0, waiting for transfers between devices: 118 us -> none  [on_device(): lax.psum_scatter(lax.dot_general(operator, left_rows, contract, preferred...]
    another operation x13 -> x2, other arithmetic: 91.3 us -> 2.48 us  [on_device(): jnp.stack([jnp.where(first, own, partner), jnp.where(first, partner, own)...]
    ppermute x0 -> x23, waiting for transfers between devices: none -> 70.5 us  [swap(): return lax.ppermute(value, axis, [(i, i ^ mask) for i in range(count)])]
    all_to_all x0 -> x3, waiting for transfers between devices: none -> 55.9 us  [the longest x1 42.1 us: on_device(): lax.all_to_all(image_term.reshape(cols, -1, image_term.shape[1]), 'col',...]
    ppermute x0 -> x23, starting transfers between devices: none -> 36.6 us  [swap(): return lax.ppermute(value, axis, [(i, i ^ mask) for i in range(count)])]
    all_to_all x0 -> x1, blocking collectives: none -> 22.9 us  [sum_everywhere(): share = lax.all_to_all(pieces, ('row', 'col'), 0, 0).sum(0)]
  transfers between devices with their start and end apart: 5 -> 26, of which waited for: 5 -> 10; matrix products, arithmetic and copies ran while one was open for 23% -> 12% of each run, Pallas kernels for 0% -> 5%
where the time goes in v1:
time: 346 us; the launch traced here: 340 us
  waiting for transfers between devices  126 us (36%)
  matrix products  51.9 us (15%)
  starting transfers between devices  51.2 us (15%)
  local copies, waits for them, and re-layouts  48.5 us (14%)
  blocking collectives  22.9 us (7%)
  other arithmetic  22.2 us (6%)
  Pallas kernels  15.8 us (5%)
    ppermute x23, waiting for transfers between devices, swap(): return lax.ppermute(value, axis, [(i, i ^ mask) for i in range(count)])  70.5 us
    all_to_all x1, waiting for transfers between devices, on_device(): lax.all_to_all(image_term.reshape(cols, -1, image_term.shape[1]), 'col',...  42.1 us
    ppermute x23, starting transfers between devices, swap(): return lax.ppermute(value, axis, [(i, i ^ mask) for i in range(count)])  36.6 us
    all_to_all x1, blocking collectives, sum_everywhere(): share = lax.all_to_all(pieces, ('row', 'col'), 0, 0).sum(0)  22.9 us
    dot_general x1, matrix products, on_device(): lax.dot_general(operator, late_rows, TRANSPOSED, preferred_element_type=j...  20.5 us
    dynamic_update_slice x23, local copies, waits for them, and re-layouts, gather_grid(): lax.dynamic_update_index_in_dim(whole, shard, (me ^ mask) >> shift, 0)  17.3 us
    pallas_call x1, Pallas kernels, factors_of(): pl.pallas_call(factor_kernel, out_shape=[jax.ShapeDtypeStruct((size, size...  15.8 us
    dot_general x1, matrix products, on_device(): jnp.dot(operator, right_rows, preferred_element_type=jnp.float32)  15.5 us
  transfers between devices with their start and end apart: 26, of which 10 were waited for; matrix products, arithmetic and copies ran while one was open for 12% of the time, Pallas kernels for 5%

profile of v1, /device:TPU:1, one launch (start us, length us, event | category | flops | bytes accessed | tf_op | source)
XLA Modules:
  0.0 339.9 jit_solution(15695353578670074944)
XLA Ops:
  0.6 3.6 %collective-permute-start.1 = (bf16[288,384]{1,0:T(8,128)(2,1)}, bf16[288,384]{1,0:T(8,128)(2,1)S(1)}, u32[]{:S(2)}, u32[]{:S(2)}) collective-permute-start(bf16[288,384]{1,0:T(8,128)(2,1)} %param.4), channel_id=1, source_target_pairs={{0,48},{8,56},{16,32},{24,40},{32,16},{40,24},{48,0},{56,8},{64,11... | collective-permute-start | bytes 663560 | tf_op jit(solution)/shard_map/ppermute | solution.py:124
  4.3 3.6 %collective-permute-start.3 = (bf16[288,384]{1,0:T(8,128)(2,1)}, bf16[288,384]{1,0:T(8,128)(2,1)S(1)}, u32[]{:S(2)}, u32[]{:S(2)}) collective-permute-start(bf16[288,384]{1,0:T(8,128)(2,1)} %param.4), channel_id=1, source_target_pairs={{0,64},{8,72},{16,80},{24,88},{32,96},{40,104},{48,112},{56,120},{... | collective-permute-start | bytes 663560 | tf_op jit(solution)/shard_map/ppermute | solution.py:124
  9.1 2.5 collective-permute-start.9
  16.9 4.3 %collective-permute-done.4 = bf16[288,384]{1,0:T(8,128)(2,1)S(1)} collective-permute-done((bf16[288,384]{1,0:T(8,128)(2,1)S(1)}, bf16[288,384]{1,0:T(8,128)(2,1)S(1)}, u32[]{:S(2)}, u32[]{:S(2)}) %collective-permute-start.4) | collective-permute-done | bytes 221216 | tf_op jit(solution)/shard_map/ppermute | solution.py:124
  23.2 4.4 %collective-permute-done.5 = bf16[288,384]{1,0:T(8,128)(2,1)S(1)} collective-permute-done((bf16[288,384]{1,0:T(8,128)(2,1)S(1)}, bf16[288,384]{1,0:T(8,128)(2,1)S(1)}, u32[]{:S(2)}, u32[]{:S(2)}) %collective-permute-start.5) | collective-permute-done | bytes 221216 | tf_op jit(solution)/shard_map/ppermute | solution.py:124
  28.1 5.8 %collective-permute-done.6 = bf16[288,384]{1,0:T(8,128)(2,1)S(1)} collective-permute-done((bf16[288,384]{1,0:T(8,128)(2,1)S(1)}, bf16[288,384]{1,0:T(8,128)(2,1)S(1)}, u32[]{:S(2)}, u32[]{:S(2)}) %collective-permute-start.6) | collective-permute-done | bytes 221216 | tf_op jit(solution)/shard_map/ppermute | solution.py:124
  34.0 9.2 %collective-permute-start.7 = (bf16[8,288,384]{2,1,0:T(8,128)(2,1)S(1)}, bf16[8,288,384]{2,1,0:T(8,128)(2,1)S(1)}, u32[]{:S(2)}, u32[]{:S(2)}) collective-permute-start(bf16[8,288,384]{2,1,0:T(8,128)(2,1)S(1)} %bitcast_dynamic-update-slice_fusion.16), channel_id=1, source_target_pairs={{0,8},{8,0},{16,24},{24,16},{32,40},{40,32},{48,56},{56,48},{64,72... | collective-permute-start | bytes 5308424 | tf_op jit(solution)/shard_map/ppermute | solution.py:124
  46.8 2.3 collective-permute-start.13
  56.7 7.2 %collective-permute-done.12 = bf16[288,576]{1,0:T(8,128)(2,1)S(1)} collective-permute-done((bf16[288,576]{1,0:T(8,128)(2,1)}, bf16[288,576]{1,0:T(8,128)(2,1)S(1)}, u32[]{:S(2)}, u32[]{:S(2)}) %collective-permute-start.12) | collective-permute-done | bytes 331808 | tf_op jit(solution)/shard_map/ppermute | solution.py:124
  70.5 15.5 %fusion.4 = (bf16[2304,384]{0,1:T(8,128)(2,1)}, f32[2304,384]{0,1:T(8,128)S(1)}) fusion(bf16[4608,384]{1,0:T(8,128)(2,1)} %bitcast.83, bf16[2304,4608]{1,0:T(8,128)(2,1)} %param.3), kind=kOutput, calls=%fused_computation.40 | convolution fusion | flops 8154611712 | bytes 30081024 | tf_op jit(solution)/shard_map/dot_general | solution.py:161
  87.8 3.7 %fusion.5 = f32[576,384]{1,0:T(8,128)S(1)} fusion(bf16[2304,576]{1,0:T(8,128)(2,1)} %bitcast.22, bf16[2304,384]{0,1:T(8,128)(2,1)S(1)} %fusion), kind=kOutput, calls=%fused_computation.41 | convolution fusion | flops 1019215872 | bytes 5308416 | tf_op jit(solution)/shard_map/dot_general | solution.py:163
  91.5 3.6 %fusion.1 = f32[576,384]{1,0:T(8,128)S(1)} fusion(bf16[2304,576]{1,0:T(8,128)(2,1)} %bitcast.22, bf16[2304,384]{0,1:T(8,128)(2,1)S(1)} %fusion, f32[2304,384]{0,1:T(8,128)S(1)} %get-tuple-element.13, bf16[2304,384]{0,1:T(8,128)(2,1)S(1)} %copy-done.1), kind=kOutput, calls=%fused_computation.8 | convolution fusion | flops 1023639552 | bytes 10616832 | tf_op jit(solution)/shard_map/dot_general | solution.py:163
  95.2 4.7 %fusion.2 = f32[576,384]{1,0:T(8,128)} fusion(f32[576,384]{1,0:T(8,128)S(1)} %fusion.1, f32[576,384]{1,0:T(8,128)S(1)} %fusion.5, bf16[2304,576]{1,0:T(8,128)(2,1)} %bitcast.22, bf16[2304,384]{0,1:T(8,128)(2,1)S(1)} %copy-done.1), kind=kOutput, calls=%fused_computation.12 | convolution fusion | flops 1019658240 | bytes 7077888 | tf_op jit(solution)/shard_map/dot_general | solution.py:163
  99.9 20.5 %convolution_bitcast_fusion = f32[4608,576]{0,1:T(8,128)} fusion(bf16[2304,576]{1,0:T(8,128)(2,1)} %bitcast.22, bf16[2304,4608]{1,0:T(8,128)(2,1)} %param.3), kind=kOutput, calls=%fused_computation | convolution fusion | flops 12230590464 | bytes 34504704 | tf_op jit(solution)/shard_map/dot_general | solution.py:171
  120.4 12.1 %copy.11 = f32[4608,576]{1,0:T(8,128)} copy(f32[4608,576]{0,1:T(8,128)} %convolution_bitcast_fusion) | data formatting | bytes 21233664 | tf_op jit(solution)/shard_map/dot_general | solution.py:171
  132.5 5.7 %dynamic-slice_bitcast_fusion = f32[8,288,576]{2,1,0:T(8,128)} fusion(f32[8,2,288,576]{3,2,1,0:T(8,128)} %bitcast.80, s32[]{:T(128)S(6)} %select_n.97), kind=kLoop, calls=%fused_computation.2 | loop fusion | bytes 10616836 | tf_op jit(solution)/shard_map/jit(dynamic_index_in_dim)/squeeze | solution.py:178
  138.8 3.4 all_to_all.21
  142.2 22.9 %all_to_all.26 = f32[128,1,1728]{2,1,0:T(1,128)} all-to-all(f32[128,1,1728]{2,1,0:T(1,128)} %all_to_all.21), channel_id=1, replica_groups=mesh['row'=16,'col'=8] {'row','col'}, dimensions={0} | all-to-all | bytes 1769472 | tf_op jit(solution)/shard_map/all_to_all | solution.py:134
  168.2 6.0 %all-to-all-start.2 = ((f32[128,1,1728]{2,1,0:T(1,128)}), f32[128,1,1728]{2,1,0:T(1,128)}, u32[]{:S(2)}, u32[]{:S(2)}) async-start(f32[128,1,1728]{2,1,0:T(1,128)} %broadcast_in_dim.100), calls=%async_computation.2 | async-start | bytes 1835008 | tf_op jit(solution)/shard_map/all_to_all | solution.py:129
  174.2 3.0 copy.9
  177.2 13.8 %all-to-all-done.2 = f32[128,1,1728]{2,1,0:T(1,128)} async-done(((f32[128,1,1728]{2,1,0:T(1,128)}), f32[128,1,1728]{2,1,0:T(1,128)}, u32[]{:S(2)}, u32[]{:S(2)}) %all-to-all-start.2) | async-done | bytes 884768 | tf_op jit(solution)/shard_map/all_to_all | solution.py:129
  190.9 3.7 %all-to-all-start = ((f32[8,288,384]{2,1,0:T(8,128)}), f32[8,288,384]{2,1,0:T(8,128)S(1)}, u32[]{:S(2)}, u32[]{:S(2)}) async-start(f32[8,288,384]{2,1,0:T(8,128)} %bitcast.82), calls=%async_computation | async-start | bytes 7077888 | tf_op jit(solution)/shard_map/all_to_all | solution.py:166
  194.6 7.6 %bitcast_add_fusion = f32[8,288,576]{2,1,0:T(8,128)} fusion(f32[8,288,576]{2,1,0:T(8,128)} %collective-permute-done.22, f32[8,2,288,576]{3,2,1,0:T(8,128)} %bitcast.81, s32[]{:T(128)S(6)} %select_n.96), kind=kLoop, calls=%fused_computation.1 | loop fusion | flops 1327104 | bytes 15925252 | tf_op jit(solution)/shard_map/add | solution.py:179
  202.2 42.1 %all-to-all-done = f32[8,288,384]{2,1,0:T(8,128)S(1)} async-done(((f32[8,288,384]{2,1,0:T(8,128)}), f32[8,288,384]{2,1,0:T(8,128)S(1)}, u32[]{:S(2)}, u32[]{:S(2)}) %all-to-all-start) | async-done | bytes 3538976 | tf_op jit(solution)/shard_map/all_to_all | solution.py:166
  246.1 4.9 %all-to-all-start.3 = ((f32[8,288,576]{2,1,0:T(8,128)}), f32[8,288,576]{2,1,0:T(8,128)}, u32[]{:S(2)}, u32[]{:S(2)}) async-start(f32[8,288,576]{2,1,0:T(8,128)} %bitcast_add_fusion), calls=%async_computation.3 | async-start | bytes 11796480 | tf_op jit(solution)/shard_map/all_to_all | solution.py:181
  251.0 3.4 reduce.1
  254.9 15.8 %shard_map.50 = (f32[384,384]{1,0:T(8,128)S(1)}, f32[576,384]{1,0:T(8,128)S(1)}) custom-call(f32[576,384]{1,0:T(8,128)S(1)} %reshape.36.core_ref), custom_call_target="tpu_custom_call" | custom-call | flops 20000000000 | bytes 3000000 | tf_op jit(solution)/shard_map/pallas_call | solution.py:109
  270.8 2.2 reduce_sum.27
  276.0 2.5 collective-permute-start.17
  279.9 40.0 %collective-permute-done.18 = bf16[288,384]{1,0:T(8,128)(2,1)S(1)} collective-permute-done((bf16[288,384]{1,0:T(8,128)(2,1)S(1)}, bf16[288,384]{1,0:T(8,128)(2,1)S(1)}, u32[]{:S(2)}, u32[]{:S(2)}) %collective-permute-start.18) | collective-permute-done | bytes 221216 | tf_op jit(solution)/shard_map/ppermute | solution.py:124
  325.4 6.7 %collective-permute-done.19 = bf16[288,384]{1,0:T(8,128)(2,1)S(1)} collective-permute-done((bf16[288,384]{1,0:T(8,128)(2,1)S(1)}, bf16[288,384]{1,0:T(8,128)(2,1)S(1)}, u32[]{:S(2)}, u32[]{:S(2)}) %collective-permute-start.19) | collective-permute-done | bytes 221216 | tf_op jit(solution)/shard_map/ppermute | solution.py:124
  334.4 3.1 reduce_sum.29
  (73 shorter events, 49.2 us)
Async XLA Ops:
  0.6 12.3 %collective-permute-start.1 = (bf16[288,384]{1,0:T(8,128)(2,1)}, bf16[288,384]{1,0:T(8,128)(2,1)S(1)}, u32[]{:S(2)}, u32[]{:S(2)}) collective-permute-start(bf16[288,384]{1,0:T(8,128)(2,1)} %param.4), channel_id=1, source_target_pairs={{0,48},{8,56},{16,32},{24,40},{32,16},{40,24},{48,0},{56,8},{64,11... | collective-permute-start | bytes 663560 | tf_op jit(solution)/shard_map/ppermute | solution.py:124
  4.3 8.5 %collective-permute-start = (bf16[288,384]{1,0:T(8,128)(2,1)}, bf16[288,384]{1,0:T(8,128)(2,1)S(1)}, u32[]{:S(2)}, u32[]{:S(2)}) collective-permute-start(bf16[288,384]{1,0:T(8,128)(2,1)} %param.4), channel_id=1, source_target_pairs={{0,16},{8,24},{16,0},{24,8},{32,48},{40,56},{48,32},{56,40},{64,80... | collective-permute-start | bytes 663560 | tf_op jit(solution)/shard_map/ppermute | solution.py:124
  4.3 9.5 %collective-permute-start.3 = (bf16[288,384]{1,0:T(8,128)(2,1)}, bf16[288,384]{1,0:T(8,128)(2,1)S(1)}, u32[]{:S(2)}, u32[]{:S(2)}) collective-permute-start(bf16[288,384]{1,0:T(8,128)(2,1)} %param.4), channel_id=1, source_target_pairs={{0,64},{8,72},{16,80},{24,88},{32,96},{40,104},{48,112},{56,120},{... | collective-permute-start | bytes 663560 | tf_op jit(solution)/shard_map/ppermute | solution.py:124
  7.9 8.1 %collective-permute-start.2 = (bf16[288,384]{1,0:T(8,128)(2,1)}, bf16[288,384]{1,0:T(8,128)(2,1)S(1)}, u32[]{:S(2)}, u32[]{:S(2)}) collective-permute-start(bf16[288,384]{1,0:T(8,128)(2,1)} %param.4), channel_id=1, source_target_pairs={{0,32},{8,40},{16,48},{24,56},{32,0},{40,8},{48,16},{56,24},{64,96... | collective-permute-start | bytes 663560 | tf_op jit(solution)/shard_map/ppermute | solution.py:124
  9.1 41.8 %collective-permute-start.9 = (bf16[288,576]{1,0:T(8,128)(2,1)}, bf16[288,576]{1,0:T(8,128)(2,1)}, u32[]{:S(2)}, u32[]{:S(2)}) collective-permute-start(bf16[288,576]{1,0:T(8,128)(2,1)} %param.5), channel_id=1, source_target_pairs={{0,6},{1,7},{2,4},{3,5},{4,2},{5,3},{6,0},{7,1},{8,14},{9,15},{10,... | collective-permute-start | bytes 995336 | tf_op jit(solution)/shard_map/ppermute | solution.py:124
  12.8 34.0 %collective-permute-start.8 = (bf16[288,576]{1,0:T(8,128)(2,1)}, bf16[288,576]{1,0:T(8,128)(2,1)}, u32[]{:S(2)}, u32[]{:S(2)}) collective-permute-start(bf16[288,576]{1,0:T(8,128)(2,1)} %param.5), channel_id=1, source_target_pairs={{0,2},{1,3},{2,0},{3,1},{4,6},{5,7},{6,4},{7,5},{8,10},{9,11},{10,... | collective-permute-start | bytes 995336 | tf_op jit(solution)/shard_map/ppermute | solution.py:124
  12.9 33.9 %collective-permute-start.11 = (bf16[288,576]{1,0:T(8,128)(2,1)}, bf16[288,576]{1,0:T(8,128)(2,1)}, u32[]{:S(2)}, u32[]{:S(2)}) collective-permute-start(bf16[288,576]{1,0:T(8,128)(2,1)} %param.5), channel_id=1, source_target_pairs={{0,1},{1,0},{2,3},{3,2},{4,5},{5,4},{6,7},{7,6},{8,9},{9,8},{10,11... | collective-permute-start | bytes 995336 | tf_op jit(solution)/shard_map/ppermute | solution.py:124
  13.8 39.4 %collective-permute-start.10 = (bf16[288,576]{1,0:T(8,128)(2,1)}, bf16[288,576]{1,0:T(8,128)(2,1)}, u32[]{:S(2)}, u32[]{:S(2)}) collective-permute-start(bf16[288,576]{1,0:T(8,128)(2,1)} %param.5), channel_id=1, source_target_pairs={{0,4},{1,5},{2,6},{3,7},{4,0},{5,1},{6,2},{7,3},{8,12},{9,13},{10,... | collective-permute-start | bytes 995336 | tf_op jit(solution)/shard_map/ppermute | solution.py:124
  16.0 5.2 %collective-permute-start.4 = (bf16[288,384]{1,0:T(8,128)(2,1)S(1)}, bf16[288,384]{1,0:T(8,128)(2,1)S(1)}, u32[]{:S(2)}, u32[]{:S(2)}) collective-permute-start(bf16[288,384]{1,0:T(8,128)(2,1)S(1)} %collective-permute-done.3), channel_id=1, source_target_pairs={{0,16},{8,24},{16,0},{24,8},{32,48},{40,56},{48,32},{56,40},{64,80... | collective-permute-start | bytes 663560 | tf_op jit(solution)/shard_map/ppermute | solution.py:124
  21.2 6.4 %collective-permute-start.5 = (bf16[288,384]{1,0:T(8,128)(2,1)S(1)}, bf16[288,384]{1,0:T(8,128)(2,1)S(1)}, u32[]{:S(2)}, u32[]{:S(2)}) collective-permute-start(bf16[288,384]{1,0:T(8,128)(2,1)S(1)} %collective-permute-done.3), channel_id=1, source_target_pairs={{0,48},{8,56},{16,32},{24,40},{32,16},{40,24},{48,0},{56,8},{64,11... | collective-permute-start | bytes 663560 | tf_op jit(solution)/shard_map/ppermute | solution.py:124
  27.6 6.4 %collective-permute-start.6 = (bf16[288,384]{1,0:T(8,128)(2,1)S(1)}, bf16[288,384]{1,0:T(8,128)(2,1)S(1)}, u32[]{:S(2)}, u32[]{:S(2)}) collective-permute-start(bf16[288,384]{1,0:T(8,128)(2,1)S(1)} %collective-permute-done.3), channel_id=1, source_target_pairs={{0,32},{8,40},{16,48},{24,56},{32,0},{40,8},{48,16},{56,24},{64,96... | collective-permute-start | bytes 663560 | tf_op jit(solution)/shard_map/ppermute | solution.py:124
  34.0 34.0 %collective-permute-start.7 = (bf16[8,288,384]{2,1,0:T(8,128)(2,1)S(1)}, bf16[8,288,384]{2,1,0:T(8,128)(2,1)S(1)}, u32[]{:S(2)}, u32[]{:S(2)}) collective-permute-start(bf16[8,288,384]{2,1,0:T(8,128)(2,1)S(1)} %bitcast_dynamic-update-slice_fusion.16), channel_id=1, source_target_pairs={{0,8},{8,0},{16,24},{24,16},{32,40},{40,32},{48,56},{56,48},{64,72... | collective-permute-start | bytes 5308424 | tf_op jit(solution)/shard_map/ppermute | solution.py:124
  46.8 20.5 %collective-permute-start.14 = (bf16[288,576]{1,0:T(8,128)(2,1)}, bf16[288,576]{1,0:T(8,128)(2,1)S(1)}, u32[]{:S(2)}, u32[]{:S(2)}) collective-permute-start(bf16[288,576]{1,0:T(8,128)(2,1)} %collective-permute-done.11), channel_id=1, source_target_pairs={{0,4},{1,5},{2,6},{3,7},{4,0},{5,1},{6,2},{7,3},{8,12},{9,13},{10,... | collective-permute-start | bytes 995336 | tf_op jit(solution)/shard_map/ppermute | solution.py:124
  46.8 19.7 %collective-permute-start.13 = (bf16[288,576]{1,0:T(8,128)(2,1)}, bf16[288,576]{1,0:T(8,128)(2,1)S(1)}, u32[]{:S(2)}, u32[]{:S(2)}) collective-permute-start(bf16[288,576]{1,0:T(8,128)(2,1)} %collective-permute-done.11), channel_id=1, source_target_pairs={{0,6},{1,7},{2,4},{3,5},{4,2},{5,3},{6,0},{7,1},{8,14},{9,15},{10,... | collective-permute-start | bytes 995336 | tf_op jit(solution)/shard_map/ppermute | solution.py:124
  50.9 12.9 %collective-permute-start.12 = (bf16[288,576]{1,0:T(8,128)(2,1)}, bf16[288,576]{1,0:T(8,128)(2,1)S(1)}, u32[]{:S(2)}, u32[]{:S(2)}) collective-permute-start(bf16[288,576]{1,0:T(8,128)(2,1)} %collective-permute-done.11), channel_id=1, source_target_pairs={{0,2},{1,3},{2,0},{3,1},{4,6},{5,7},{6,4},{7,5},{8,10},{9,11},{10,... | collective-permute-start | bytes 995336 | tf_op jit(solution)/shard_map/ppermute | solution.py:124
  87.8 3.7 %copy-start.1 = (bf16[2304,384]{0,1:T(8,128)(2,1)S(1)}, bf16[2304,384]{0,1:T(8,128)(2,1)}, u32[]{:S(2)}) copy-start(bf16[2304,384]{0,1:T(8,128)(2,1)} %get-tuple-element.12) | copy-start | bytes 5308420
  138.1 56.5 %collective-permute-start.22 = (f32[8,288,576]{2,1,0:T(8,128)}, f32[8,288,576]{2,1,0:T(8,128)}, u32[]{:S(2)}, u32[]{:S(2)}) collective-permute-start(f32[8,288,576]{2,1,0:T(8,128)} %dynamic-slice_bitcast_fusion), channel_id=1, source_target_pairs={{0,8},{8,0},{16,24},{24,16},{32,40},{40,32},{48,56},{56,48},{64,72... | collective-permute-start | bytes 15925256 | tf_op jit(solution)/shard_map/ppermute | solution.py:124
  168.2 22.7 %all-to-all-start.2 = ((f32[128,1,1728]{2,1,0:T(1,128)}), f32[128,1,1728]{2,1,0:T(1,128)}, u32[]{:S(2)}, u32[]{:S(2)}) async-start(f32[128,1,1728]{2,1,0:T(1,128)} %broadcast_in_dim.100), calls=%async_computation.2 | async-start | bytes 1835008 | tf_op jit(solution)/shard_map/all_to_all | solution.py:129
  190.9 53.4 %all-to-all-start = ((f32[8,288,384]{2,1,0:T(8,128)}), f32[8,288,384]{2,1,0:T(8,128)S(1)}, u32[]{:S(2)}, u32[]{:S(2)}) async-start(f32[8,288,384]{2,1,0:T(8,128)} %bitcast.82), calls=%async_computation | async-start | bytes 7077888 | tf_op jit(solution)/shard_map/all_to_all | solution.py:166
  244.3 1.8 copy-start
  246.1 88.3 %all-to-all-start.3 = ((f32[8,288,576]{2,1,0:T(8,128)}), f32[8,288,576]{2,1,0:T(8,128)}, u32[]{:S(2)}, u32[]{:S(2)}) async-start(f32[8,288,576]{2,1,0:T(8,128)} %bitcast_add_fusion), calls=%async_computation.3 | async-start | bytes 11796480 | tf_op jit(solution)/shard_map/all_to_all | solution.py:181
  276.0 43.9 %collective-permute-start.18 = (bf16[288,384]{1,0:T(8,128)(2,1)S(1)}, bf16[288,384]{1,0:T(8,128)(2,1)S(1)}, u32[]{:S(2)}, u32[]{:S(2)}) collective-permute-start(bf16[288,384]{1,0:T(8,128)(2,1)S(1)} %get-tuple-element.15), channel_id=1, source_target_pairs={{0,1},{1,0},{2,3},{3,2},{4,5},{5,4},{6,7},{7,6},{8,9},{9,8},{10,11... | collective-permute-start | bytes 663560 | tf_op jit(solution)/shard_map/ppermute | solution.py:124
  276.0 45.7 %collective-permute-start.15 = (bf16[288,384]{1,0:T(8,128)(2,1)S(1)}, bf16[288,384]{1,0:T(8,128)(2,1)S(1)}, u32[]{:S(2)}, u32[]{:S(2)}) collective-permute-start(bf16[288,384]{1,0:T(8,128)(2,1)S(1)} %get-tuple-element.15), channel_id=1, source_target_pairs={{0,2},{1,3},{2,0},{3,1},{4,6},{5,7},{6,4},{7,5},{8,10},{9,11},{10,... | collective-permute-start | bytes 663560 | tf_op jit(solution)/shard_map/ppermute | solution.py:124
  276.0 48.0 %collective-permute-start.17 = (bf16[288,384]{1,0:T(8,128)(2,1)S(1)}, bf16[288,384]{1,0:T(8,128)(2,1)S(1)}, u32[]{:S(2)}, u32[]{:S(2)}) collective-permute-start(bf16[288,384]{1,0:T(8,128)(2,1)S(1)} %get-tuple-element.15), channel_id=1, source_target_pairs={{0,4},{1,5},{2,6},{3,7},{4,0},{5,1},{6,2},{7,3},{8,12},{9,13},{10,... | collective-permute-start | bytes 663560 | tf_op jit(solution)/shard_map/ppermute | solution.py:124
  278.6 44.7 %collective-permute-start.16 = (bf16[288,384]{1,0:T(8,128)(2,1)S(1)}, bf16[288,384]{1,0:T(8,128)(2,1)S(1)}, u32[]{:S(2)}, u32[]{:S(2)}) collective-permute-start(bf16[288,384]{1,0:T(8,128)(2,1)S(1)} %get-tuple-element.15), channel_id=1, source_target_pairs={{0,6},{1,7},{2,4},{3,5},{4,2},{5,3},{6,0},{7,1},{8,14},{9,15},{10,... | collective-permute-start | bytes 663560 | tf_op jit(solution)/shard_map/ppermute | solution.py:124
  319.9 13.7 %collective-permute-start.21 = (bf16[288,384]{1,0:T(8,128)(2,1)S(1)}, bf16[288,384]{1,0:T(8,128)(2,1)S(1)}, u32[]{:S(2)}, u32[]{:S(2)}) collective-permute-start(bf16[288,384]{1,0:T(8,128)(2,1)S(1)} %collective-permute-done.18), channel_id=1, source_target_pairs={{0,4},{1,5},{2,6},{3,7},{4,0},{5,1},{6,2},{7,3},{8,12},{9,13},{10,... | collective-permute-start | bytes 663560 | tf_op jit(solution)/shard_map/ppermute | solution.py:124
  319.9 13.0 %collective-permute-start.20 = (bf16[288,384]{1,0:T(8,128)(2,1)S(1)}, bf16[288,384]{1,0:T(8,128)(2,1)S(1)}, u32[]{:S(2)}, u32[]{:S(2)}) collective-permute-start(bf16[288,384]{1,0:T(8,128)(2,1)S(1)} %collective-permute-done.18), channel_id=1, source_target_pairs={{0,6},{1,7},{2,4},{3,5},{4,2},{5,3},{6,0},{7,1},{8,14},{9,15},{10,... | collective-permute-start | bytes 663560 | tf_op jit(solution)/shard_map/ppermute | solution.py:124
  321.7 10.4 %collective-permute-start.19 = (bf16[288,384]{1,0:T(8,128)(2,1)S(1)}, bf16[288,384]{1,0:T(8,128)(2,1)S(1)}, u32[]{:S(2)}, u32[]{:S(2)}) collective-permute-start(bf16[288,384]{1,0:T(8,128)(2,1)S(1)} %collective-permute-done.18), channel_id=1, source_target_pairs={{0,2},{1,3},{2,0},{3,1},{4,6},{5,7},{6,4},{7,5},{8,10},{9,11},{10,... | collective-permute-start | bytes 663560 | tf_op jit(solution)/shard_map/ppermute | solution.py:124

commit v2 on v1

--- a/solution.py
+++ b/solution.py
@@ -16,16 +16,6 @@
 TRANSPOSED = (((0,), (0,)), ((), ()))
 CORE, ROW_RING, ROW_Z = 1, (2, 6, 4), 8
 COL_RING, COL_Z = (2, 6, 4), 1
-
-
-def three_parts(value):
-    high_part = value.astype(jnp.bfloat16)
-    rest = value - lax.optimization_barrier(high_part).astype(jnp.float32)
-    middle_part = rest.astype(jnp.bfloat16)
-    low_part = (rest - lax.optimization_barrier(middle_part).astype(jnp.float32)).astype(
-        jnp.bfloat16
-    )
-    return high_part, middle_part, low_part
 
 
 def kernel_parts(value):
@@ -77,8 +67,10 @@
 
 
 def factor_kernel(core_ref, lower_inverse_ref, ortho_ref, block_ref):
-    core = core_ref[...]
-    size = core.shape[1]
+    tall, size = ortho_ref.shape
+    core = jnp.concatenate(
+        [core_ref[at * tall : (at + 1) * tall, :] for at in range(size // BLOCK)], 1
+    )
     work = lower_inverse_ref
     dot = functools.partial(
         lax.dot_general, precision=HIGHEST, preferred_element_type=jnp.float32
@@ -104,8 +96,7 @@
     ortho_ref[...] = dot(core, work[...], (((1,), (1,)), ((), ())))
 
 
-def factors_of(core):
-    tall, size = core.shape
+def factors_of(core, tall, size):
     return pl.pallas_call(
         factor_kernel,
         out_shape=[
@@ -124,63 +115,265 @@
     return lax.ppermute(value, axis, [(i, i ^ mask) for i in range(count)])
 
 
-def gather_direct(value, axes, count):
-    copies = jnp.broadcast_to(value[None], (count,) + value.shape)
-    return lax.all_to_all(copies, axes, 0, 0)
-
-
-def sum_everywhere(value, count):
-    pieces = value.reshape(count, -1)
-    share = lax.all_to_all(pieces, ("row", "col"), 0, 0).sum(0)
-    return gather_direct(share, ("row", "col"), count).reshape(value.shape)
-
-
-def gather_grid(value, axis, count, ring, across, shift):
-    me = lax.axis_index(axis)
-    other = swap(value, axis, count, across)
-    found = [(0, value)] + [(mask, swap(value, axis, count, mask)) for mask in ring]
-    found += [(across, other)]
-    found += [(across ^ mask, swap(other, axis, count, mask)) for mask in ring]
-    whole = jnp.zeros((len(found),) + value.shape, value.dtype)
-    for mask, shard in found:
-        whole = lax.dynamic_update_index_in_dim(whole, shard, (me ^ mask) >> shift, 0)
-    return whole
+def image_kernel(place_ref, operator_ref, own_ref, other_ref, *refs):
+    image_ref, upper_refs, near_ref, far_ref, right_ref = refs[0], refs[1:5], *refs[5:]
+
+    @pl.when(pl.program_id(0) == 0)
+    def _():
+        core_place = place_ref[0] & 1
+        shard = own_ref.shape[1]
+        for k in range(own_ref.shape[0]):
+            for ref, place in ((own_ref, core_place), (other_ref, 1 - core_place)):
+                start = pl.multiple_of((2 * k + place) * shard, shard)
+                right_ref[pl.ds(start, shard), :] = ref[k]
+
+    image = jnp.dot(operator_ref[...], right_ref[...], preferred_element_type=jnp.float32)
+    half = image.shape[0] // 2
+    first = (place_ref[1] & 1) == 0
+    near = jnp.where(first, image[:half], image[half:])
+    far = jnp.where(first, image[half:], image[:half])
+    image_ref[0], image_ref[1] = near, far
+    near_ref[0], far_ref[0] = near[half // 2 :], far[half // 2 :]
+    for k, ref in enumerate(upper_refs):
+
+        @pl.when(pl.program_id(0) == k)
+        def _(ref=ref):
+            ref[0], ref[1] = near[: half // 2], far[: half // 2]
+
+
+def image_term(places, operator, own, other):
+    height, width = operator.shape
+    shard, size = own.shape[1:]
+    tile, part = 2 * shard, shard // 2
+    shards = pl.BlockSpec(own.shape, lambda i, place: (0, 0, 0))
+    grid_spec = pltpu.PrefetchScalarGridSpec(
+        num_scalar_prefetch=1,
+        grid=(height // tile,),
+        in_specs=[
+            pl.BlockSpec((tile, width), lambda i, place: ((place[1] >> 1) ^ i, 0)),
+            shards,
+            shards,
+        ],
+        out_specs=[pl.BlockSpec((2, shard, size), lambda i, place: (i, 0, 0))]
+        + [pl.BlockSpec((2, part, size), lambda i, place: (0, 0, 0))] * 4
+        + [pl.BlockSpec((1, part, size), lambda i, place: (i, 0, 0))] * 2,
+        scratch_shapes=[pltpu.VMEM((width, size), jnp.bfloat16)],
+    )
+    return pl.pallas_call(
+        image_kernel,
+        grid_spec=grid_spec,
+        out_shape=[
+            jax.ShapeDtypeStruct(shape, jnp.float32)
+            for shape in [(height // shard, shard, size)]
+            + [(2, part, size)] * 4
+            + [(height // tile, part, size)] * 2
+        ],
+        compiler_params=pltpu.CompilerParams(vmem_limit_bytes=56 * 2**20),
+        cost_estimate=pl.CostEstimate(
+            flops=12 * 10**9, bytes_accessed=30 * 10**6, transcendentals=0
+        ),
+    )(places, operator, own, other)
+
+
+def core_kernel(place_ref, image_ref, *refs):
+    left_refs = refs[:8]
+    core_ref, left_out_ref, total_ref = refs[8:]
+    step = pl.program_id(0)
+    shard = image_ref.shape[1]
+    starts = [pl.multiple_of((place_ref[1] ^ mask) * shard, shard) for mask in range(8)]
+
+    @pl.when(step == 0)
+    def _():
+        for start, ref in zip(starts, left_refs):
+            left_out_ref[pl.ds(start, shard), :] = ref[...]
+        total_ref[...] = jnp.zeros_like(total_ref)
+
+    parts, lefts = [], []
+    for k in range(2):
+        start = pl.multiple_of((place_ref[1] ^ (2 * step + k)) * shard, shard)
+        left = left_out_ref[pl.ds(start, shard), :]
+        lefts.append(left)
+        parts.append(jnp.concatenate(kernel_parts(image_ref[k]), 1).astype(jnp.bfloat16))
+    sums = lax.dot_general(
+        jnp.concatenate(lefts, 0),
+        jnp.concatenate(parts, 0),
+        TRANSPOSED,
+        preferred_element_type=jnp.float32,
+    )
+    size = total_ref.shape[1]
+    total_ref[...] += sums[:, :size] + (sums[:, size : 2 * size] + sums[:, 2 * size :])
+
+    @pl.when(step == pl.num_programs(0) - 1)
+    def _():
+        tall, size = total_ref.shape
+        for at in range(size // BLOCK):
+            core_ref[at * tall : (at + 1) * tall, :] = total_ref[
+                :, at * BLOCK : (at + 1) * BLOCK
+            ]
+        used = tall * size // BLOCK
+        core_ref[used:, :] = jnp.zeros((core_ref.shape[0] - used, BLOCK), jnp.float32)
+
+
+def core_of(places, image, left_shards, shares):
+    count, shard, size = image.shape
+    tall = left_shards[0].shape[1]
+    grid_spec = pltpu.PrefetchScalarGridSpec(
+        num_scalar_prefetch=1,
+        grid=(count // 2,),
+        in_specs=[pl.BlockSpec((2, shard, size), lambda i, place: (i, 0, 0))]
+        + [pl.BlockSpec((shard, tall), lambda i, place: (0, 0))] * count,
+        out_specs=[
+            pl.BlockSpec((shares * 16, BLOCK), lambda i, place: (0, 0)),
+            pl.BlockSpec((count * shard, tall), lambda i, place: (0, 0)),
+        ],
+        scratch_shapes=[pltpu.VMEM((tall, size), jnp.float32)],
+    )
+    return pl.pallas_call(
+        core_kernel,
+        grid_spec=grid_spec,
+        out_shape=[
+            jax.ShapeDtypeStruct((shares * 16, BLOCK), jnp.float32),
+            jax.ShapeDtypeStruct((count * shard, tall), jnp.bfloat16),
+        ],
+        compiler_params=pltpu.CompilerParams(vmem_limit_bytes=56 * 2**20),
+        cost_estimate=pl.CostEstimate(
+            flops=4 * 10**9, bytes_accessed=7 * 10**6, transcendentals=0
+        ),
+    )(places, image, *left_shards)
+
+
+def wide_kernel(place_ref, operator_ref, left_ref, *refs):
+    outs, left_t_ref = refs[:4], refs[4]
+    shard = 2 * outs[0].shape[1]
+    core_place, y_low = place_ref[0] & 1, (place_ref[0] >> 1) & 1
+
+    @pl.when(pl.program_id(0) == 0)
+    def _():
+        left_t_ref[...] = left_ref[...].T
+
+    wide = jnp.dot(left_t_ref[...], operator_ref[...], preferred_element_type=jnp.float32).T
+    pieces = [wide[k * shard : (k + 1) * shard, :] for k in range(4)]
+    first_core, first_y = core_place == 0, y_low == 0
+    for which in range(2):
+        of_core = [
+            jnp.where(first_core, pieces[2 * y + which], pieces[2 * y + 1 - which])
+            for y in range(2)
+        ]
+        for slot in range(2):
+            piece = jnp.where(first_y, of_core[slot], of_core[1 - slot])
+            outs[2 * which][slot] = piece[: shard // 2, :]
+            outs[2 * which + 1][slot] = piece[shard // 2 :, :]
+
+
+def wide_terms(places, operator, left_rows, shard):
+    height, width = operator.shape
+    tall = left_rows.shape[1]
+    steps, half = width // (4 * shard), shard // 2
+    grid_spec = pltpu.PrefetchScalarGridSpec(
+        num_scalar_prefetch=1,
+        grid=(steps,),
+        in_specs=[
+            pl.BlockSpec((height, 4 * shard), lambda j, place: (0, (place[0] >> 2) ^ j)),
+            pl.BlockSpec((height, tall), lambda j, place: (0, 0)),
+        ],
+        out_specs=[pl.BlockSpec((2, half, tall), lambda j, place: (j, 0, 0))] * 4,
+        scratch_shapes=[pltpu.VMEM((tall, height), jnp.bfloat16)],
+    )
+    return pl.pallas_call(
+        wide_kernel,
+        grid_spec=grid_spec,
+        out_shape=[jax.ShapeDtypeStruct((2 * steps, half, tall), jnp.float32)] * 4,
+        compiler_params=pltpu.CompilerParams(vmem_limit_bytes=56 * 2**20),
+        cost_estimate=pl.CostEstimate(
+            flops=13 * 10**9, bytes_accessed=35 * 10**6, transcendentals=0
+        ),
+    )(places, operator, left_rows)
+
+
+def sum_shares(value, count):
+    return lax.all_to_all(value.reshape(count, -1, BLOCK), ("row", "col"), 0, 0).sum(0)
+
+
+def gather_shares(share, count):
+    copies = jnp.broadcast_to(share[None], (count,) + share.shape)
+    return lax.all_to_all(copies, ("row", "col"), 0, 0).reshape(-1, share.shape[-1])
+
+
+def scatter_first(upper, lower, far, axis, count, ring, across):
+    sends = [swap(pair, axis, count, mask) for pair, mask in zip(upper[1:], ring)]
+    return upper[0], sends, lower, swap(far, axis, count, across)
+
+
+def scatter_last(state, axis, count, ring, across):
+    own, sends, lower, crossed = state
+    upper_far = own[1] + sum(send[1] for send in sends)
+    upper_sum = own[0] + sum(send[0] for send in sends)
+    upper_sum = upper_sum + swap(upper_far, axis, count, across)
+    lower_sum = lower[0] + crossed[0]
+    for k in range(1, 4):
+        at = ring[k - 1] >> 1 if axis == "col" else k
+        lower_sum = lower_sum + swap(lower[k] + crossed[at], axis, count, ring[k - 1])
+    return jnp.concatenate([upper_sum, lower_sum], 0)
 
 
 def on_device(rows, cols, operator, sketch_right, sketch_left):
-    core_index = lax.axis_index("row") & 1
-    own = gather_grid(sketch_right, "row", rows, ROW_RING, ROW_Z, 1)
-    partner = swap(own, "row", rows, CORE)
-    first = core_index == 0
-    right_rows = jnp.stack(
-        [jnp.where(first, own, partner), jnp.where(first, partner, own)], 1
-    ).reshape(-1, sketch_right.shape[1])
-    left_rows = gather_grid(sketch_left, "col", cols, COL_RING, COL_Z, 0)
-    left_rows = left_rows.reshape(-1, sketch_left.shape[1])
-
-    image_term = jnp.dot(operator, right_rows, preferred_element_type=jnp.float32)
-    core_term = sum(
-        lax.dot_general(left_rows, part, TRANSPOSED, preferred_element_type=jnp.float32)
-        for part in three_parts(image_term)
-    )
-    image_piece = lax.all_to_all(
-        image_term.reshape(cols, -1, image_term.shape[1]), "col", 0, 0
-    ).sum(0)
-
-    core_term, late_rows = lax.optimization_barrier((core_term, left_rows))
-    wide_term = lax.dot_general(
-        operator, late_rows, TRANSPOSED, preferred_element_type=jnp.float32
-    )
-    core = sum_everywhere(core_term, rows * cols)
-
-    halves = wide_term.reshape(rows // 2, 2, -1, wide_term.shape[1])
-    mine = lax.dynamic_index_in_dim(halves, core_index, 1, False)
-    theirs = lax.dynamic_index_in_dim(halves, 1 - core_index, 1, False)
-    paired = mine + swap(theirs, "row", rows, CORE)
+    places = jnp.stack([lax.axis_index("row"), lax.axis_index("col")]).astype(jnp.int32)
+    shard = sketch_right.shape[0]
+    join = lax.optimization_barrier
+    row_axis = ("row", rows, ROW_RING, ROW_Z)
+    col_axis = ("col", cols, COL_RING, COL_Z)
+
+    left_far = swap(sketch_left, "col", cols, COL_Z)
+    left_near = [swap(sketch_left, "col", cols, mask) for mask in COL_RING]
     same_core = [[i for i in range(rows) if i % 2 == c] for c in range(2)]
-    wide_piece = lax.all_to_all(paired, "row", 0, 0, axis_index_groups=same_core).sum(0)
-
-    lower_inverse, ortho = factors_of(core)
+    own = lax.all_to_all(
+        jnp.broadcast_to(sketch_right[None], (rows // 2,) + sketch_right.shape),
+        "row",
+        0,
+        0,
+        axis_index_groups=same_core,
+    )
+    own, left_far, left_near = join((own, left_far, left_near))
+    left_beyond = [swap(left_far, "col", cols, mask) for mask in COL_RING]
+    image, *messages = image_term(places, operator, own, swap(own, "row", rows, CORE))
+    image, messages, left_beyond = join((image, messages, left_beyond))
+    left_shards = {0: sketch_left, COL_Z: left_far}
+    left_shards.update(zip(COL_RING, left_near))
+    left_shards.update((COL_Z ^ mask, shard) for mask, shard in zip(COL_RING, left_beyond))
+    core_term, left_rows = core_of(
+        places, image, [left_shards[mask] for mask in range(cols)], rows * cols
+    )
+
+    core_share = sum_shares(core_term, rows * cols)
+    upper, near, far = [messages[mask >> 1] for mask in (0, *COL_RING)], *messages[4:]
+    image_state = scatter_first(
+        upper, [near[mask >> 1] for mask in (0, *COL_RING)], far, *col_axis
+    )
+    wide_pieces = wide_terms(places, operator, left_rows, shard)
+    core_share, wide_pieces = join((core_share, wide_pieces))
+
+    core = gather_shares(core_share, rows * cols)
+    mine_upper, mine_lower, other_upper, other_lower = wide_pieces
+    other_upper = swap(other_upper, "row", rows, CORE)
+    other_lower = swap(other_lower, "row", rows, CORE)
+    order = [mask >> 1 for mask in (0, *ROW_RING)]
+    upper = [
+        jnp.stack([mine_upper[k] + other_upper[k], mine_upper[4 ^ k] + other_upper[4 ^ k]])
+        for k in order
+    ]
+    lower = [mine_lower[k] + other_lower[k] for k in order]
+    far = jnp.stack([mine_lower[4 ^ k] + other_lower[4 ^ k] for k in order])
+    core, upper, lower, far, image_state = join((core, upper, lower, far, image_state))
+
+    wide_state = scatter_first(upper, lower, far, *row_axis)
+    image_piece = scatter_last(image_state, *col_axis)
+    tall, size = sketch_left.shape[1], sketch_right.shape[1]
+    lower_inverse, ortho = factors_of(core, tall, size)
+    wide_state, image_piece, lower_inverse, ortho = join(
+        (wide_state, image_piece, lower_inverse, ortho)
+    )
+
+    wide_piece = scatter_last(wide_state, *row_axis)
     factor = math.sqrt(N * L)
     left_piece = (
         factor
@@ -192,8 +385,9 @@
             preferred_element_type=jnp.float32,
         )
     ).astype(jnp.bfloat16)
-    left_factor = gather_grid(left_piece, "col", cols, COL_RING, COL_Z, 0)
-    left_factor = left_factor.reshape(-1, left_piece.shape[1])
+    left_factor = lax.all_to_all(
+        jnp.broadcast_to(left_piece[None], (cols,) + left_piece.shape), "col", 0, 0
+    ).reshape(-1, size)
     right_factor = jnp.dot(wide_piece, ortho, precision=HIGHEST).astype(jnp.bfloat16)
     return (left_factor, right_factor)
 

time: 346 us -> 235 us (0.68); the launches traced: 340 us -> 234 us
  waiting for transfers between devices: 126 us -> 67.9 us
  Pallas kernels: 15.8 us -> 66.3 us
  matrix products: 51.9 us -> 3.16 us
  local copies, waits for them, and re-layouts: 48.5 us -> 10.4 us
  blocking collectives: 22.9 us -> 0 us
  starting transfers between devices: 51.2 us -> 68.4 us
  other arithmetic: 22.2 us -> 17 us
    all_to_all x3 -> x4, waiting for transfers between devices: 55.9 us -> 0.01 us  [the longest x1 0.01 us: on_device(): lax.all_to_all(jnp.broadcast_to(sketch_right[None], (rows // 2,) + sketch...]
    pallas_call x0 -> x3, Pallas kernels: none -> 50.6 us  [the longest x1 22 us: wide_terms(): pl.pallas_call(wide_kernel, grid_spec=grid_spec, out_shape=[jax.ShapeDtyp...]
    dot_general x5 -> x0, matrix products: 48 us -> none  [the longest x1 20.5 us: on_device(): lax.dot_general(operator, late_rows, TRANSPOSED, preferred_element_type=j...]
    all_to_all x1 -> x0, blocking collectives: 22.9 us -> none  [sum_everywhere(): share = lax.all_to_all(pieces, ('row', 'col'), 0, 0).sum(0)]
    dynamic_update_slice x23 -> x0, local copies, waits for them, and re-layouts: 17.3 us -> none  [gather_grid(): lax.dynamic_update_index_in_dim(whole, shard, (me ^ mask) >> shift, 0)]
    all_to_all x3 -> x4, starting transfers between devices: 14.5 us -> 31.3 us  [the longest x1 10.2 us: sum_shares(): lax.all_to_all(value.reshape(count, -1, BLOCK), ('row', 'col'), 0, 0).sum(0)]
    dot_general x2 -> x0, local copies, waits for them, and re-layouts: 15 us -> none  [the longest x1 12.1 us: on_device(): lax.dot_general(operator, late_rows, TRANSPOSED, preferred_element_type=j...]
    reduce_sum x3 -> x1, other arithmetic: 7.02 us -> 0.14 us  [sum_shares(): lax.all_to_all(value.reshape(count, -1, BLOCK), ('row', 'col'), 0, 0).sum(0)]
  transfers between devices with their start and end apart: 26 -> 30, of which waited for: 10 -> 6; matrix products, arithmetic and copies ran while one was open for 12% -> 8% of each run, Pallas kernels for 5% -> 24%
where the time goes in v2:
time: 235 us; the launch traced here: 234 us
  starting transfers between devices  68.4 us (29%)
  waiting for transfers between devices  67.9 us (29%)
  Pallas kernels  66.3 us (28%)
  other arithmetic  17 us (7%)
  local copies, waits for them, and re-layouts  10.4 us (4%)
  matrix products  3.16 us (1%)
    ppermute x26, waiting for transfers between devices, swap(): return lax.ppermute(value, axis, [(i, i ^ mask) for i in range(count)])  67.9 us
    ppermute x26, starting transfers between devices, swap(): return lax.ppermute(value, axis, [(i, i ^ mask) for i in range(count)])  37 us
    pallas_call x1, Pallas kernels, wide_terms(): pl.pallas_call(wide_kernel, grid_spec=grid_spec, out_shape=[jax.ShapeDtyp...  22 us
    pallas_call x1, Pallas kernels, image_term(): pl.pallas_call(image_kernel, grid_spec=grid_spec, out_shape=[jax.ShapeDty...  18.3 us
    pallas_call x1, Pallas kernels, factors_of(): pl.pallas_call(factor_kernel, out_shape=[jax.ShapeDtypeStruct((size, size...  15.6 us
    pallas_call x1, Pallas kernels, core_of(): pl.pallas_call(core_kernel, grid_spec=grid_spec, out_shape=[jax.ShapeDtyp...  10.4 us
    all_to_all x1, starting transfers between devices, sum_shares(): lax.all_to_all(value.reshape(count, -1, BLOCK), ('row', 'col'), 0, 0).sum(0)  10.2 us
    all_to_all x1, starting transfers between devices, on_device(): lax.all_to_all(jnp.broadcast_to(sketch_right[None], (rows // 2,) + sketch...  8.46 us
  transfers between devices with their start and end apart: 30, of which 6 were waited for; matrix products, arithmetic and copies ran while one was open for 8% of the time, Pallas kernels for 24%

profile of v2, /device:TPU:1, one launch (start us, length us, event | category | flops | bytes accessed | tf_op | source)
XLA Modules:
  0.0 234.2 jit_solution(6502182695088653046)
XLA Ops:
  0.6 2.3 broadcast_in_dim.6
  2.9 8.5 %all-to-all-start = ((bf16[8,288,384]{2,1,0:T(8,128)(2,1)}), bf16[8,288,384]{2,1,0:T(8,128)(2,1)S(1)}, u32[]{:S(2)}, u32[]{:S(2)}) async-start(bf16[8,288,384]{2,1,0:T(8,128)(2,1)} %broadcast_in_dim.6), calls=%async_computation | async-start | bytes 3538944 | tf_op jit(solution)/shard_map/all_to_all | solution.py:329
  13.4 1.8 collective-permute-start.2
  15.9 23.4 %collective-permute-done.refs_1_ = bf16[288,576]{1,0:T(8,128)(2,1)S(1)} collective-permute-done((bf16[288,576]{1,0:T(8,128)(2,1)S(1)}, bf16[288,576]{1,0:T(8,128)(2,1)S(1)}, u32[]{:S(2)}, u32[]{:S(2)}) %collective-permute-start) | collective-permute-done | bytes 331808 | tf_op jit(solution)/shard_map/ppermute | solution.py:115
  39.3 1.6 collective-permute-start.4
  42.8 1.8 collective-permute-start.6
  45.2 18.3 %shard_map.50 = (f32[8,288,384]{2,1,0:T(8,128)}, f32[2,144,384]{2,1,0:T(8,128)}, f32[2,144,384]{2,1,0:T(8,128)}, f32[2,144,384]{2,1,0:T(8,128)}, f32[2,144,384]{...) custom-call(s32[2]{0:T(128)} %pad_add_fusion.place_ref, bf16[2304,4608]{1,0:T(8,128)(2,1)} %operator_ref.3, ...), custom_call_target="tpu_custom_call" | custom-call | flops 12000000000 | bytes 30000000 | tf_op jit(solution)/shard_map/pallas_call | solution.py:162
  64.5 10.4 %shard_map.51 = (f32[2048,128]{1,0:T(8,128)}, bf16[2304,576]{1,0:T(8,128)(2,1)}) custom-call(s32[2]{0:T(128)} %pad_add_fusion.place_ref, f32[8,288,384]{2,1,0:T(8,128)} %get-tuple-element.77.image_ref, bf16[288,576]{1,0:T(8,128)(2,1)} %refs_0_.1, bf16[288,576]{1,0:T(8,128)(2,1)} %copy-done.22, bf16[288,576]{1,0:T(8,128)(2,1)} %copy-done.23, ...), custom_call_target="tpu_custom_call" | custom-call | flops 4000000000 | bytes 7000000 | tf_op jit(solution)/shard_map/pallas_call | solution.py:231
  74.9 10.2 %all-to-all-start.1 = ((f32[128,16,128]{2,1,0:T(8,128)}), f32[128,16,128]{2,1,0:T(8,128)S(1)}, u32[]{:S(2)}, u32[]{:S(2)}) async-start(f32[128,16,128]{2,1,0:T(8,128)} %bitcast.61), calls=%async_computation.1 | async-start | bytes 2097152 | tf_op jit(solution)/shard_map/all_to_all | solution.py:294
  85.1 22.0 %shard_map.52 = (f32[8,144,576]{2,1,0:T(8,128)}, f32[8,144,576]{2,1,0:T(8,128)}, f32[8,144,576]{2,1,0:T(8,128)}, f32[8,144,576]{2,1,0:T(8,128)}) custom-call(s32[2]{0:T(128)} %pad_add_fusion.place_ref, bf16[2304,4608]{1,0:T(8,128)(2,1)} %operator_ref.3, bf16[2304,576]{1,0:T(8,128)(2,1)} %get-tuple-element.85.left_ref), custom_call_target="tpu_custom_call" | custom-call | flops 12999999488 | bytes 35000000 | tf_op jit(solution)/shard_map/pallas_call | solution.py:282
  110.5 1.8 collective-permute-start.11
  114.3 8.4 %all-to-all-start.2 = ((f32[128,16,128]{2,1,0:T(8,128)}), f32[128,16,128]{2,1,0:T(8,128)S(1)}, u32[]{:S(2)}, u32[]{:S(2)}) async-start(f32[128,16,128]{2,1,0:T(8,128)} %broadcast_in_dim.7), calls=%async_computation.2 | async-start | bytes 2097152 | tf_op jit(solution)/shard_map/all_to_all | solution.py:299
  122.7 3.0 %collective-permute-start.12 = (f32[2,144,384]{2,1,0:T(8,128)}, f32[2,144,384]{2,1,0:T(8,128)S(1)}, u32[]{:S(2)}, u32[]{:S(2)}) collective-permute-start(f32[2,144,384]{2,1,0:T(8,128)} %get-tuple-element.98), channel_id=1, source_target_pairs={{0,4},{1,5},{2,6},{3,7},{4,0},{5,1},{6,2},{7,3},{8,12},{9,13},{10,... | collective-permute-start | bytes 1327112 | tf_op jit(solution)/shard_map/ppermute | solution.py:115
  125.7 4.0 %slice_add_fusion.3 = (f32[1,144,576]{2,1,0:T(8,128)S(1)}, f32[1,144,576]{2,1,0:T(8,128)S(1)}, f32[1,144,576]{2,1,0:T(8,128)S(1)}, f32[1,144,576]{2,1,0:T(8,128)...) fusion(f32[8,144,576]{2,1,0:T(8,128)} %collective-permute-done.9, ...), kind=kLoop, calls=%fused_computation.15 | loop fusion | flops 663552 | bytes 7962624 | tf_op jit(solution)/shard_map/add | solution.py:365
  129.7 2.1 slice_add_fusion.9
  135.2 11.3 %collective-permute-done.12 = f32[2,144,384]{2,1,0:T(8,128)S(1)} collective-permute-done((f32[2,144,384]{2,1,0:T(8,128)}, f32[2,144,384]{2,1,0:T(8,128)S(1)}, u32[]{:S(2)}, u32[]{:S(2)}) %collective-permute-start.12) | collective-permute-done | bytes 442400 | tf_op jit(solution)/shard_map/ppermute | solution.py:115
  147.2 1.6 add_bitcast_fusion.1
  148.9 1.4 collective-permute-start.18
  151.9 4.0 %collective-permute-start.20 = (f32[144,384]{1,0:T(8,128)S(1)}, f32[144,384]{1,0:T(8,128)S(1)}, u32[]{:S(2)}, u32[]{:S(2)}) collective-permute-start(f32[144,384]{1,0:T(8,128)S(1)} %get-tuple-element.155), channel_id=1, source_target_pairs={{0,6},{1,7},{2,4},{3,5},{4,2},{5,3},{6,0},{7,1},{8,14},{9,15},{10,... | collective-permute-start | bytes 663560 | tf_op jit(solution)/shard_map/ppermute | solution.py:115
  155.9 1.2 collective-permute-start.17
  158.7 1.9 collective-permute-start.16
  160.5 15.6 %shard_map.53 = (f32[384,384]{1,0:T(8,128)S(1)}, f32[576,384]{1,0:T(8,128)S(1)}) custom-call(f32[2048,128]{1,0:T(8,128)S(1)} %bitcast.60), custom_call_target="tpu_custom_call" | custom-call | flops 20000000000 | bytes 3000000 | tf_op jit(solution)/shard_map/pallas_call | solution.py:100
  178.5 4.3 %collective-permute-done.21 = f32[144,384]{1,0:T(8,128)S(1)} collective-permute-done((f32[144,384]{1,0:T(8,128)S(1)}, f32[144,384]{1,0:T(8,128)S(1)}, u32[]{:S(2)}, u32[]{:S(2)}) %collective-permute-start.21) | collective-permute-done | bytes 221216 | tf_op jit(solution)/shard_map/ppermute | solution.py:115
  183.9 6.1 %collective-permute-done.16 = f32[2,144,576]{2,1,0:T(8,128)S(1)} collective-permute-done((f32[2,144,576]{2,1,0:T(8,128)S(1)}, f32[2,144,576]{2,1,0:T(8,128)S(1)}, u32[]{:S(2)}, u32[]{:S(2)}) %collective-permute-start.16) | collective-permute-done | bytes 663584 | tf_op jit(solution)/shard_map/ppermute | solution.py:115
  192.0 1.4 broadcast_in_dim.8
  193.3 4.3 %all-to-all-start.3 = ((bf16[8,288,384]{2,1,0:T(8,128)(2,1)}), bf16[8,288,384]{2,1,0:T(8,128)(2,1)}, u32[]{:S(2)}, u32[]{:S(2)}) async-start(bf16[8,288,384]{2,1,0:T(8,128)(2,1)} %broadcast_in_dim.8), calls=%async_computation.3 | async-start | bytes 3538944 | tf_op jit(solution)/shard_map/all_to_all | solution.py:388
  197.6 1.4 add_bitcast_fusion
  199.1 4.2 %collective-permute-start.22 = (f32[144,576]{1,0:T(8,128)S(1)}, f32[144,576]{1,0:T(8,128)S(1)}, u32[]{:S(2)}, u32[]{:S(2)}) collective-permute-start(f32[144,576]{1,0:T(8,128)S(1)} %add_bitcast_fusion), channel_id=1, source_target_pairs={{0,64},{8,72},{16,80},{24,88},{32,96},{40,104},{48,112},{56,120},{... | collective-permute-start | bytes 995336 | tf_op jit(solution)/shard_map/ppermute | solution.py:115
  204.0 2.8 %collective-permute-start.25 = (f32[144,576]{1,0:T(8,128)S(1)}, f32[144,576]{1,0:T(8,128)S(1)}, u32[]{:S(2)}, u32[]{:S(2)}) collective-permute-start(f32[144,576]{1,0:T(8,128)S(1)} %get-tuple-element.151), channel_id=1, source_target_pairs={{0,32},{8,40},{16,48},{24,56},{32,0},{40,8},{48,16},{56,24},{64,96... | collective-permute-start | bytes 995336 | tf_op jit(solution)/shard_map/ppermute | solution.py:115
  206.8 22.0 %collective-permute-done.22 = f32[144,576]{1,0:T(8,128)S(1)} collective-permute-done((f32[144,576]{1,0:T(8,128)S(1)}, f32[144,576]{1,0:T(8,128)S(1)}, u32[]{:S(2)}, u32[]{:S(2)}) %collective-permute-start.22) | collective-permute-done | bytes 331808 | tf_op jit(solution)/shard_map/ppermute | solution.py:115
  229.1 2.2 convolution_convert_fusion
  231.3 2.9 %copy.6 = bf16[2304,384]{1,0:T(8,128)(2,1)} copy(bf16[2304,384]{1,0:T(8,128)(2,1)} %bitcast.18) | data formatting | bytes 3538944
  (111 shorter events, 25.1 us)
Async XLA Ops:
  2.9 36.4 %all-to-all-start = ((bf16[8,288,384]{2,1,0:T(8,128)(2,1)}), bf16[8,288,384]{2,1,0:T(8,128)(2,1)S(1)}, u32[]{:S(2)}, u32[]{:S(2)}) async-start(bf16[8,288,384]{2,1,0:T(8,128)(2,1)} %broadcast_in_dim.6), calls=%async_computation | async-start | bytes 3538944 | tf_op jit(solution)/shard_map/all_to_all | solution.py:329
  11.4 27.9 %collective-permute-start = (bf16[288,576]{1,0:T(8,128)(2,1)S(1)}, bf16[288,576]{1,0:T(8,128)(2,1)S(1)}, u32[]{:S(2)}, u32[]{:S(2)}) collective-permute-start(bf16[288,576]{1,0:T(8,128)(2,1)S(1)} %copy-done.21), channel_id=1, source_target_pairs={{0,1},{1,0},{2,3},{3,2},{4,5},{5,4},{6,7},{7,6},{8,9},{9,8},{10,11... | collective-permute-start | bytes 995336 | tf_op jit(solution)/shard_map/ppermute | solution.py:115
  12.2 27.1 %collective-permute-start.1 = (bf16[288,576]{1,0:T(8,128)(2,1)S(1)}, bf16[288,576]{1,0:T(8,128)(2,1)S(1)}, u32[]{:S(2)}, u32[]{:S(2)}) collective-permute-start(bf16[288,576]{1,0:T(8,128)(2,1)S(1)} %copy-done.21), channel_id=1, source_target_pairs={{0,2},{1,3},{2,0},{3,1},{4,6},{5,7},{6,4},{7,5},{8,10},{9,11},{10,... | collective-permute-start | bytes 995336 | tf_op jit(solution)/shard_map/ppermute | solution.py:115
  13.4 25.9 %collective-permute-start.2 = (bf16[288,576]{1,0:T(8,128)(2,1)S(1)}, bf16[288,576]{1,0:T(8,128)(2,1)S(1)}, u32[]{:S(2)}, u32[]{:S(2)}) collective-permute-start(bf16[288,576]{1,0:T(8,128)(2,1)S(1)} %copy-done.21), channel_id=1, source_target_pairs={{0,6},{1,7},{2,4},{3,5},{4,2},{5,3},{6,0},{7,1},{8,14},{9,15},{10,... | collective-permute-start | bytes 995336 | tf_op jit(solution)/shard_map/ppermute | solution.py:115
  15.2 24.1 %collective-permute-start.3 = (bf16[288,576]{1,0:T(8,128)(2,1)S(1)}, bf16[288,576]{1,0:T(8,128)(2,1)}, u32[]{:S(2)}, u32[]{:S(2)}) collective-permute-start(bf16[288,576]{1,0:T(8,128)(2,1)S(1)} %copy-done.21), channel_id=1, source_target_pairs={{0,4},{1,5},{2,6},{3,7},{4,0},{5,1},{6,2},{7,3},{8,12},{9,13},{10,... | collective-permute-start | bytes 995336 | tf_op jit(solution)/shard_map/ppermute | solution.py:115
  39.3 5.9 %collective-permute-start.4 = (bf16[8,288,384]{2,1,0:T(8,128)(2,1)S(1)}, bf16[8,288,384]{2,1,0:T(8,128)(2,1)}, u32[]{:S(2)}, u32[]{:S(2)}) collective-permute-start(bf16[8,288,384]{2,1,0:T(8,128)(2,1)S(1)} %all-to-all-done.own_ref), channel_id=1, source_target_pairs={{0,8},{8,0},{16,24},{24,16},{32,40},{40,32},{48,56},{56,48},{64,72... | collective-permute-start | bytes 5308424 | tf_op jit(solution)/shard_map/ppermute | solution.py:115
  41.5 22.0 %collective-permute-start.5 = (bf16[288,576]{1,0:T(8,128)(2,1)S(1)}, bf16[288,576]{1,0:T(8,128)(2,1)S(1)}, u32[]{:S(2)}, u32[]{:S(2)}) collective-permute-start(bf16[288,576]{1,0:T(8,128)(2,1)S(1)} %collective-permute-done.refs_1_), channel_id=1, source_target_pairs={{0,2},{1,3},{2,0},{3,1},{4,6},{5,7},{6,4},{7,5},{8,10},{9,11},{10,... | collective-permute-start | bytes 995336 | tf_op jit(solution)/shard_map/ppermute | solution.py:115
  42.8 20.8 %collective-permute-start.6 = (bf16[288,576]{1,0:T(8,128)(2,1)S(1)}, bf16[288,576]{1,0:T(8,128)(2,1)S(1)}, u32[]{:S(2)}, u32[]{:S(2)}) collective-permute-start(bf16[288,576]{1,0:T(8,128)(2,1)S(1)} %collective-permute-done.refs_1_), channel_id=1, source_target_pairs={{0,6},{1,7},{2,4},{3,5},{4,2},{5,3},{6,0},{7,1},{8,14},{9,15},{10,... | collective-permute-start | bytes 995336 | tf_op jit(solution)/shard_map/ppermute | solution.py:115
  44.6 19.0 %collective-permute-start.7 = (bf16[288,576]{1,0:T(8,128)(2,1)S(1)}, bf16[288,576]{1,0:T(8,128)(2,1)S(1)}, u32[]{:S(2)}, u32[]{:S(2)}) collective-permute-start(bf16[288,576]{1,0:T(8,128)(2,1)S(1)} %collective-permute-done.refs_1_), channel_id=1, source_target_pairs={{0,4},{1,5},{2,6},{3,7},{4,0},{5,1},{6,2},{7,3},{8,12},{9,13},{10,... | collective-permute-start | bytes 995336 | tf_op jit(solution)/shard_map/ppermute | solution.py:115
  74.9 32.1 %all-to-all-start.1 = ((f32[128,16,128]{2,1,0:T(8,128)}), f32[128,16,128]{2,1,0:T(8,128)S(1)}, u32[]{:S(2)}, u32[]{:S(2)}) async-start(f32[128,16,128]{2,1,0:T(8,128)} %bitcast.61), calls=%async_computation.1 | async-start | bytes 2097152 | tf_op jit(solution)/shard_map/all_to_all | solution.py:294
  107.2 15.5 %collective-permute-start.9 = (f32[8,144,576]{2,1,0:T(8,128)}, f32[8,144,576]{2,1,0:T(8,128)}, u32[]{:S(2)}, u32[]{:S(2)}) collective-permute-start(f32[8,144,576]{2,1,0:T(8,128)} %get-tuple-element.94), channel_id=1, source_target_pairs={{0,8},{8,0},{16,24},{24,16},{32,40},{40,32},{48,56},{56,48},{64,72... | collective-permute-start | bytes 7962632 | tf_op jit(solution)/shard_map/ppermute | solution.py:115
  108.4 21.3 %collective-permute-start.8 = (f32[8,144,576]{2,1,0:T(8,128)}, f32[8,144,576]{2,1,0:T(8,128)}, u32[]{:S(2)}, u32[]{:S(2)}) collective-permute-start(f32[8,144,576]{2,1,0:T(8,128)} %get-tuple-element.92), channel_id=1, source_target_pairs={{0,8},{8,0},{16,24},{24,16},{32,40},{40,32},{48,56},{56,48},{64,72... | collective-permute-start | bytes 7962632 | tf_op jit(solution)/shard_map/ppermute | solution.py:115
  108.5 38.7 %collective-permute-start.13 = (f32[4,144,384]{2,1,0:T(8,128)}, f32[4,144,384]{2,1,0:T(8,128)S(1)}, u32[]{:S(2)}, u32[]{:S(2)}) collective-permute-start(f32[4,144,384]{2,1,0:T(8,128)} %get-tuple-element.100), channel_id=1, source_target_pairs={{0,1},{1,0},{2,3},{3,2},{4,5},{5,4},{6,7},{7,6},{8,9},{9,8},{10,11... | collective-permute-start | bytes 2654216 | tf_op jit(solution)/shard_map/ppermute | solution.py:115
  109.3 25.8 %collective-permute-start.10 = (f32[2,144,384]{2,1,0:T(8,128)}, f32[2,144,384]{2,1,0:T(8,128)}, u32[]{:S(2)}, u32[]{:S(2)}) collective-permute-start(f32[2,144,384]{2,1,0:T(8,128)} %get-tuple-element.96), channel_id=1, source_target_pairs={{0,2},{1,3},{2,0},{3,1},{4,6},{5,7},{6,4},{7,5},{8,10},{9,11},{10,... | collective-permute-start | bytes 1327112 | tf_op jit(solution)/shard_map/ppermute | solution.py:115
  110.5 24.7 %collective-permute-start.11 = (f32[2,144,384]{2,1,0:T(8,128)}, f32[2,144,384]{2,1,0:T(8,128)}, u32[]{:S(2)}, u32[]{:S(2)}) collective-permute-start(f32[2,144,384]{2,1,0:T(8,128)} %get-tuple-element.97), channel_id=1, source_target_pairs={{0,6},{1,7},{2,4},{3,5},{4,2},{5,3},{6,0},{7,1},{8,14},{9,15},{10,... | collective-permute-start | bytes 1327112 | tf_op jit(solution)/shard_map/ppermute | solution.py:115
  114.3 32.9 %all-to-all-start.2 = ((f32[128,16,128]{2,1,0:T(8,128)}), f32[128,16,128]{2,1,0:T(8,128)S(1)}, u32[]{:S(2)}, u32[]{:S(2)}) async-start(f32[128,16,128]{2,1,0:T(8,128)} %broadcast_in_dim.7), calls=%async_computation.2 | async-start | bytes 2097152 | tf_op jit(solution)/shard_map/all_to_all | solution.py:299
  122.7 23.7 %collective-permute-start.12 = (f32[2,144,384]{2,1,0:T(8,128)}, f32[2,144,384]{2,1,0:T(8,128)S(1)}, u32[]{:S(2)}, u32[]{:S(2)}) collective-permute-start(f32[2,144,384]{2,1,0:T(8,128)} %get-tuple-element.98), channel_id=1, source_target_pairs={{0,4},{1,5},{2,6},{3,7},{4,0},{5,1},{6,2},{7,3},{8,12},{9,13},{10,... | collective-permute-start | bytes 1327112 | tf_op jit(solution)/shard_map/ppermute | solution.py:115
  148.9 8.6 %collective-permute-start.18 = (f32[144,384]{1,0:T(8,128)S(1)}, f32[144,384]{1,0:T(8,128)S(1)}, u32[]{:S(2)}, u32[]{:S(2)}) collective-permute-start(f32[144,384]{1,0:T(8,128)S(1)} %add_bitcast_fusion.1), channel_id=1, source_target_pairs={{0,1},{1,0},{2,3},{3,2},{4,5},{5,4},{6,7},{7,6},{8,9},{9,8},{10,11... | collective-permute-start | bytes 663560 | tf_op jit(solution)/shard_map/ppermute | solution.py:115
  151.5 7.1 %collective-permute-start.19 = (f32[144,384]{1,0:T(8,128)S(1)}, f32[144,384]{1,0:T(8,128)S(1)}, u32[]{:S(2)}, u32[]{:S(2)}) collective-permute-start(f32[144,384]{1,0:T(8,128)S(1)} %get-tuple-element.153), channel_id=1, source_target_pairs={{0,2},{1,3},{2,0},{3,1},{4,6},{5,7},{6,4},{7,5},{8,10},{9,11},{10,... | collective-permute-start | bytes 663560 | tf_op jit(solution)/shard_map/ppermute | solution.py:115
  151.9 30.9 %copy-start.8 = (f32[144,384]{1,0:T(8,128)S(1)}, f32[144,384]{1,0:T(8,128)}, u32[]{:S(2)}) copy-start(f32[144,384]{1,0:T(8,128)} %get-tuple-element.114) | copy-start | bytes 663556
  151.9 24.2 %collective-permute-start.20 = (f32[144,384]{1,0:T(8,128)S(1)}, f32[144,384]{1,0:T(8,128)S(1)}, u32[]{:S(2)}, u32[]{:S(2)}) collective-permute-start(f32[144,384]{1,0:T(8,128)S(1)} %get-tuple-element.155), channel_id=1, source_target_pairs={{0,6},{1,7},{2,4},{3,5},{4,2},{5,3},{6,0},{7,1},{8,14},{9,15},{10,... | collective-permute-start | bytes 663560 | tf_op jit(solution)/shard_map/ppermute | solution.py:115
  155.9 34.9 %collective-permute-start.17 = (f32[4,144,576]{2,1,0:T(8,128)}, f32[4,144,576]{2,1,0:T(8,128)S(1)}, u32[]{:S(2)}, u32[]{:S(2)}) collective-permute-start(f32[4,144,576]{2,1,0:T(8,128)} %pad_maximum_fusion), channel_id=1, source_target_pairs={{0,64},{8,72},{16,80},{24,88},{32,96},{40,104},{48,112},{56,120},{... | collective-permute-start | bytes 3981320 | tf_op jit(solution)/shard_map/ppermute | solution.py:115
  157.2 26.7 %collective-permute-start.14 = (f32[2,144,576]{2,1,0:T(8,128)S(1)}, f32[2,144,576]{2,1,0:T(8,128)S(1)}, u32[]{:S(2)}, u32[]{:S(2)}) collective-permute-start(f32[2,144,576]{2,1,0:T(8,128)S(1)} %copy-done.17), channel_id=1, source_target_pairs={{0,16},{8,24},{16,0},{24,8},{32,48},{40,56},{48,32},{56,40},{64,80... | collective-permute-start | bytes 1990664 | tf_op jit(solution)/shard_map/ppermute | solution.py:115
  157.5 26.4 %collective-permute-start.15 = (f32[2,144,576]{2,1,0:T(8,128)S(1)}, f32[2,144,576]{2,1,0:T(8,128)S(1)}, u32[]{:S(2)}, u32[]{:S(2)}) collective-permute-start(f32[2,144,576]{2,1,0:T(8,128)S(1)} %copy-done.16), channel_id=1, source_target_pairs={{0,48},{8,56},{16,32},{24,40},{32,16},{40,24},{48,0},{56,8},{64,11... | collective-permute-start | bytes 1990664 | tf_op jit(solution)/shard_map/ppermute | solution.py:115
  158.7 31.3 %collective-permute-start.16 = (f32[2,144,576]{2,1,0:T(8,128)S(1)}, f32[2,144,576]{2,1,0:T(8,128)S(1)}, u32[]{:S(2)}, u32[]{:S(2)}) collective-permute-start(f32[2,144,576]{2,1,0:T(8,128)S(1)} %copy-done.15), channel_id=1, source_target_pairs={{0,32},{8,40},{16,48},{24,56},{32,0},{40,8},{48,16},{56,24},{64,96... | collective-permute-start | bytes 1990664 | tf_op jit(solution)/shard_map/ppermute | solution.py:115
  176.2 6.7 %collective-permute-start.21 = (f32[144,384]{1,0:T(8,128)S(1)}, f32[144,384]{1,0:T(8,128)S(1)}, u32[]{:S(2)}, u32[]{:S(2)}) collective-permute-start(f32[144,384]{1,0:T(8,128)S(1)} %get-tuple-element.154), channel_id=1, source_target_pairs={{0,4},{1,5},{2,6},{3,7},{4,0},{5,1},{6,2},{7,3},{8,12},{9,13},{10,... | collective-permute-start | bytes 663560 | tf_op jit(solution)/shard_map/ppermute | solution.py:115
  193.3 38.0 %all-to-all-start.3 = ((bf16[8,288,384]{2,1,0:T(8,128)(2,1)}), bf16[8,288,384]{2,1,0:T(8,128)(2,1)}, u32[]{:S(2)}, u32[]{:S(2)}) async-start(bf16[8,288,384]{2,1,0:T(8,128)(2,1)} %broadcast_in_dim.8), calls=%async_computation.3 | async-start | bytes 3538944 | tf_op jit(solution)/shard_map/all_to_all | solution.py:388
  199.1 29.7 %copy-start.10 = (f32[2,144,576]{2,1,0:T(8,128)S(1)}, f32[2,144,576]{2,1,0:T(8,128)}, u32[]{:S(2)}) copy-start(f32[2,144,576]{2,1,0:T(8,128)} %copy-done.9) | copy-start | bytes 1990660
  199.1 29.7 %collective-permute-start.22 = (f32[144,576]{1,0:T(8,128)S(1)}, f32[144,576]{1,0:T(8,128)S(1)}, u32[]{:S(2)}, u32[]{:S(2)}) collective-permute-start(f32[144,576]{1,0:T(8,128)S(1)} %add_bitcast_fusion), channel_id=1, source_target_pairs={{0,64},{8,72},{16,80},{24,88},{32,96},{40,104},{48,112},{56,120},{... | collective-permute-start | bytes 995336 | tf_op jit(solution)/shard_map/ppermute | solution.py:115
  203.5 25.5 %collective-permute-start.23 = (f32[144,576]{1,0:T(8,128)S(1)}, f32[144,576]{1,0:T(8,128)S(1)}, u32[]{:S(2)}, u32[]{:S(2)}) collective-permute-start(f32[144,576]{1,0:T(8,128)S(1)} %get-tuple-element.150), channel_id=1, source_target_pairs={{0,16},{8,24},{16,0},{24,8},{32,48},{40,56},{48,32},{56,40},{64,80... | collective-permute-start | bytes 995336 | tf_op jit(solution)/shard_map/ppermute | solution.py:115
  203.6 25.4 %collective-permute-start.24 = (f32[144,576]{1,0:T(8,128)S(1)}, f32[144,576]{1,0:T(8,128)S(1)}, u32[]{:S(2)}, u32[]{:S(2)}) collective-permute-start(f32[144,576]{1,0:T(8,128)S(1)} %get-tuple-element.152), channel_id=1, source_target_pairs={{0,48},{8,56},{16,32},{24,40},{32,16},{40,24},{48,0},{56,8},{64,11... | collective-permute-start | bytes 995336 | tf_op jit(solution)/shard_map/ppermute | solution.py:115
  204.0 25.0 %collective-permute-start.25 = (f32[144,576]{1,0:T(8,128)S(1)}, f32[144,576]{1,0:T(8,128)S(1)}, u32[]{:S(2)}, u32[]{:S(2)}) collective-permute-start(f32[144,576]{1,0:T(8,128)S(1)} %get-tuple-element.151), channel_id=1, source_target_pairs={{0,32},{8,40},{16,48},{24,56},{32,0},{40,8},{48,16},{56,24},{64,96... | collective-permute-start | bytes 995336 | tf_op jit(solution)/shard_map/ppermute | solution.py:115
  (26 other events, 331.0 us)

commit v3 on v2

--- a/solution.py
+++ b/solution.py
@@ -350,7 +350,7 @@
         upper, [near[mask >> 1] for mask in (0, *COL_RING)], far, *col_axis
     )
     wide_pieces = wide_terms(places, operator, left_rows, shard)
-    core_share, wide_pieces = join((core_share, wide_pieces))
+    core_share, wide_pieces, image_state = join((core_share, wide_pieces, image_state))
 
     core = gather_shares(core_share, rows * cols)
     mine_upper, mine_lower, other_upper, other_lower = wide_pieces

time: 235 us -> 233 us (level)
  starting transfers between devices: 68.4 us -> 64.8 us
  local copies, waits for them, and re-layouts: 10.4 us -> 13.7 us
    ppermute x26, waiting for transfers between devices: 67.9 us -> 59.6 us  [swap(): return lax.ppermute(value, axis, [(i, i ^ mask) for i in range(count)])]
    all_to_all x1, waiting for transfers between devices: 0.01 us -> 7.75 us  [gather_shares(): lax.all_to_all(copies, ('row', 'col'), 0, 0).reshape(-1, share.shape[-1])]
    ppermute x26, starting transfers between devices: 37 us -> 30.5 us  [swap(): return lax.ppermute(value, axis, [(i, i ^ mask) for i in range(count)])]
    unnamed x57 -> x67, local copies, waits for them, and re-layouts: 4.77 us -> 8.06 us
    all_to_all x1, starting transfers between devices: 4.31 us -> 7.55 us  [on_device(): lax.all_to_all(jnp.broadcast_to(left_piece[None], (cols,) + left_piece.sh...]
  transfers between devices with their start and end apart: 30 -> 30, of which waited for: 6 -> 8; matrix products, arithmetic and copies ran while one was open for 8% -> 8% of each run, Pallas kernels for 24% -> 24%
where the time goes in v3:
time: 233 us; the launch traced here: 232 us
  waiting for transfers between devices  67.4 us (29%)
  Pallas kernels  66.3 us (28%)
  starting transfers between devices  64.8 us (28%)
  other arithmetic  15.5 us (7%)
  local copies, waits for them, and re-layouts  13.7 us (6%)
  matrix products  3.16 us (1%)
    ppermute x26, waiting for transfers between devices, swap(): return lax.ppermute(value, axis, [(i, i ^ mask) for i in range(count)])  59.6 us
    ppermute x26, starting transfers between devices, swap(): return lax.ppermute(value, axis, [(i, i ^ mask) for i in range(count)])  30.5 us
    pallas_call x1, Pallas kernels, wide_terms(): pl.pallas_call(wide_kernel, grid_spec=grid_spec, out_shape=[jax.ShapeDtyp...  21.9 us
    pallas_call x1, Pallas kernels, image_term(): pl.pallas_call(image_kernel, grid_spec=grid_spec, out_shape=[jax.ShapeDty...  18.3 us
    pallas_call x1, Pallas kernels, factors_of(): pl.pallas_call(factor_kernel, out_shape=[jax.ShapeDtypeStruct((size, size...  15.6 us
    pallas_call x1, Pallas kernels, core_of(): pl.pallas_call(core_kernel, grid_spec=grid_spec, out_shape=[jax.ShapeDtyp...  10.4 us
    all_to_all x1, starting transfers between devices, sum_shares(): lax.all_to_all(value.reshape(count, -1, BLOCK), ('row', 'col'), 0, 0).sum(0)  10.2 us
    all_to_all x1, starting transfers between devices, on_device(): lax.all_to_all(jnp.broadcast_to(sketch_right[None], (rows // 2,) + sketch...  8.46 us
  transfers between devices with their start and end apart: 30, of which 8 were waited for; matrix products, arithmetic and copies ran while one was open for 8% of the time, Pallas kernels for 24%

profile of v3, /device:TPU:1, one launch (start us, length us, event | category | flops | bytes accessed | tf_op | source)
XLA Modules:
  0.0 231.8 jit_solution(10270840566028178446)
XLA Ops:
  0.6 2.3 broadcast_in_dim.6
  2.9 8.5 %all-to-all-start = ((bf16[8,288,384]{2,1,0:T(8,128)(2,1)}), bf16[8,288,384]{2,1,0:T(8,128)(2,1)S(1)}, u32[]{:S(2)}, u32[]{:S(2)}) async-start(bf16[8,288,384]{2,1,0:T(8,128)(2,1)} %broadcast_in_dim.6), calls=%async_computation | async-start | bytes 3538944 | tf_op jit(solution)/shard_map/all_to_all | solution.py:329
  13.4 1.8 collective-permute-start.2
  15.9 23.4 %collective-permute-done.refs_1_ = bf16[288,576]{1,0:T(8,128)(2,1)S(1)} collective-permute-done((bf16[288,576]{1,0:T(8,128)(2,1)S(1)}, bf16[288,576]{1,0:T(8,128)(2,1)S(1)}, u32[]{:S(2)}, u32[]{:S(2)}) %collective-permute-start) | collective-permute-done | bytes 331808 | tf_op jit(solution)/shard_map/ppermute | solution.py:115
  40.9 1.6 collective-permute-start.4
  44.4 1.8 collective-permute-start.6
  48.1 18.3 %shard_map.50 = (f32[8,288,384]{2,1,0:T(8,128)}, f32[2,144,384]{2,1,0:T(8,128)}, f32[2,144,384]{2,1,0:T(8,128)}, f32[2,144,384]{2,1,0:T(8,128)}, f32[2,144,384]{...) custom-call(s32[2]{0:T(128)} %pad_add_fusion.place_ref, bf16[2304,4608]{1,0:T(8,128)(2,1)} %operator_ref.3, ...), custom_call_target="tpu_custom_call" | custom-call | flops 12000000000 | bytes 30000000 | tf_op jit(solution)/shard_map/pallas_call | solution.py:162
  67.5 10.4 %shard_map.51 = (f32[2048,128]{1,0:T(8,128)}, bf16[2304,576]{1,0:T(8,128)(2,1)}) custom-call(s32[2]{0:T(128)} %pad_add_fusion.place_ref, f32[8,288,384]{2,1,0:T(8,128)} %get-tuple-element.86.image_ref, bf16[288,576]{1,0:T(8,128)(2,1)} %refs_0_.1, bf16[288,576]{1,0:T(8,128)(2,1)} %copy-done.27, bf16[288,576]{1,0:T(8,128)(2,1)} %copy-done.28, ...), custom_call_target="tpu_custom_call" | custom-call | flops 4000000000 | bytes 7000000 | tf_op jit(solution)/shard_map/pallas_call | solution.py:231
  77.9 10.2 %all-to-all-start.1 = ((f32[128,16,128]{2,1,0:T(8,128)}), f32[128,16,128]{2,1,0:T(8,128)S(1)}, u32[]{:S(2)}, u32[]{:S(2)}) async-start(f32[128,16,128]{2,1,0:T(8,128)} %bitcast.61), calls=%async_computation.1 | async-start | bytes 2097152 | tf_op jit(solution)/shard_map/all_to_all | solution.py:294
  88.1 1.6 collective-permute-start.11
  89.7 2.7 %collective-permute-start.10 = (f32[2,144,384]{2,1,0:T(8,128)}, f32[2,144,384]{2,1,0:T(8,128)S(1)}, u32[]{:S(2)}, u32[]{:S(2)}) collective-permute-start(f32[2,144,384]{2,1,0:T(8,128)} %get-tuple-element.102), channel_id=1, source_target_pairs={{0,4},{1,5},{2,6},{3,7},{4,0},{5,1},{6,2},{7,3},{8,12},{9,13},{10,... | collective-permute-start | bytes 1327112 | tf_op jit(solution)/shard_map/ppermute | solution.py:115
  93.3 21.9 %shard_map.52 = (f32[8,144,576]{2,1,0:T(8,128)}, f32[8,144,576]{2,1,0:T(8,128)}, f32[8,144,576]{2,1,0:T(8,128)}, f32[8,144,576]{2,1,0:T(8,128)}) custom-call(s32[2]{0:T(128)} %pad_add_fusion.place_ref, bf16[2304,4608]{1,0:T(8,128)(2,1)} %operator_ref.3, bf16[2304,576]{1,0:T(8,128)(2,1)} %get-tuple-element.94.left_ref), custom_call_target="tpu_custom_call" | custom-call | flops 12999999488 | bytes 35000000 | tf_op jit(solution)/shard_map/pallas_call | solution.py:282
  116.3 3.5 %collective-permute-done.8 = f32[2,144,384]{2,1,0:T(8,128)S(1)} collective-permute-done((f32[2,144,384]{2,1,0:T(8,128)}, f32[2,144,384]{2,1,0:T(8,128)S(1)}, u32[]{:S(2)}, u32[]{:S(2)}) %collective-permute-start.8) | collective-permute-done | bytes 442400 | tf_op jit(solution)/shard_map/ppermute | solution.py:115
  119.8 1.4 collective-permute-done.9
  123.3 8.1 %all-to-all-start.2 = ((f32[128,16,128]{2,1,0:T(8,128)}), f32[128,16,128]{2,1,0:T(8,128)S(1)}, u32[]{:S(2)}, u32[]{:S(2)}) async-start(f32[128,16,128]{2,1,0:T(8,128)} %broadcast_in_dim.7), calls=%async_computation.2 | async-start | bytes 2097152 | tf_op jit(solution)/shard_map/all_to_all | solution.py:299
  131.5 3.8 %slice_add_fusion.3 = (f32[1,144,576]{2,1,0:T(8,128)S(1)}, f32[1,144,576]{2,1,0:T(8,128)S(1)}, f32[1,144,576]{2,1,0:T(8,128)S(1)}, f32[1,144,576]{2,1,0:T(8,128)...) fusion(f32[8,144,576]{2,1,0:T(8,128)} %collective-permute-done.13, ...), kind=kLoop, calls=%fused_computation.15 | loop fusion | flops 663552 | bytes 7962624 | tf_op jit(solution)/shard_map/add | solution.py:365
  137.7 2.1 slice_add_fusion.9
  141.9 7.7 %all-to-all-done.2 = f32[128,16,128]{2,1,0:T(8,128)S(1)} async-done(((f32[128,16,128]{2,1,0:T(8,128)}), f32[128,16,128]{2,1,0:T(8,128)S(1)}, u32[]{:S(2)}, u32[]{:S(2)}) %all-to-all-start.2) | async-done | bytes 1048608 | tf_op jit(solution)/shard_map/all_to_all | solution.py:299
  149.7 1.4 add_bitcast_fusion.1
  153.4 1.9 collective-permute-start.20
  156.9 1.9 collective-permute-start.15
  160.0 15.6 %shard_map.53 = (f32[384,384]{1,0:T(8,128)S(1)}, f32[576,384]{1,0:T(8,128)S(1)}) custom-call(f32[2048,128]{1,0:T(8,128)S(1)} %bitcast.60), custom_call_target="tpu_custom_call" | custom-call | flops 20000000000 | bytes 3000000 | tf_op jit(solution)/shard_map/pallas_call | solution.py:100
  175.7 3.1 %collective-permute-start.21 = (f32[144,384]{1,0:T(8,128)S(1)}, f32[144,384]{1,0:T(8,128)S(1)}, u32[]{:S(2)}, u32[]{:S(2)}) collective-permute-start(f32[144,384]{1,0:T(8,128)S(1)} %get-tuple-element.172), channel_id=1, source_target_pairs={{0,4},{1,5},{2,6},{3,7},{4,0},{5,1},{6,2},{7,3},{8,12},{9,13},{10,... | collective-permute-start | bytes 663560 | tf_op jit(solution)/shard_map/ppermute | solution.py:115
  178.8 3.5 %collective-permute-done.21 = f32[144,384]{1,0:T(8,128)S(1)} collective-permute-done((f32[144,384]{1,0:T(8,128)S(1)}, f32[144,384]{1,0:T(8,128)S(1)}, u32[]{:S(2)}, u32[]{:S(2)}) %collective-permute-start.21) | collective-permute-done | bytes 221216 | tf_op jit(solution)/shard_map/ppermute | solution.py:115
  183.4 5.6 %collective-permute-done.16 = f32[2,144,576]{2,1,0:T(8,128)S(1)} collective-permute-done((f32[2,144,576]{2,1,0:T(8,128)S(1)}, f32[2,144,576]{2,1,0:T(8,128)S(1)}, u32[]{:S(2)}, u32[]{:S(2)}) %collective-permute-start.16) | collective-permute-done | bytes 663584 | tf_op jit(solution)/shard_map/ppermute | solution.py:115
  190.5 1.4 broadcast_in_dim.8
  191.9 7.6 %all-to-all-start.3 = ((bf16[8,288,384]{2,1,0:T(8,128)(2,1)}), bf16[8,288,384]{2,1,0:T(8,128)(2,1)}, u32[]{:S(2)}, u32[]{:S(2)}) async-start(bf16[8,288,384]{2,1,0:T(8,128)(2,1)} %broadcast_in_dim.8), calls=%async_computation.3 | async-start | bytes 3538944 | tf_op jit(solution)/shard_map/all_to_all | solution.py:388
  199.5 1.3 add_bitcast_fusion
  202.4 2.3 collective-permute-start.25
  204.7 21.8 %collective-permute-done.22 = f32[144,576]{1,0:T(8,128)S(1)} collective-permute-done((f32[144,576]{1,0:T(8,128)S(1)}, f32[144,576]{1,0:T(8,128)S(1)}, u32[]{:S(2)}, u32[]{:S(2)}) %collective-permute-start.22) | collective-permute-done | bytes 331808 | tf_op jit(solution)/shard_map/ppermute | solution.py:115
  226.8 2.2 convolution_convert_fusion
  229.0 2.9 %copy.6 = bf16[2304,384]{1,0:T(8,128)(2,1)} copy(bf16[2304,384]{1,0:T(8,128)(2,1)} %bitcast.18) | data formatting | bytes 3538944
  (121 shorter events, 27.3 us)
Async XLA Ops:
  2.9 38.0 %all-to-all-start = ((bf16[8,288,384]{2,1,0:T(8,128)(2,1)}), bf16[8,288,384]{2,1,0:T(8,128)(2,1)S(1)}, u32[]{:S(2)}, u32[]{:S(2)}) async-start(bf16[8,288,384]{2,1,0:T(8,128)(2,1)} %broadcast_in_dim.6), calls=%async_computation | async-start | bytes 3538944 | tf_op jit(solution)/shard_map/all_to_all | solution.py:329
  11.4 27.9 %collective-permute-start = (bf16[288,576]{1,0:T(8,128)(2,1)S(1)}, bf16[288,576]{1,0:T(8,128)(2,1)S(1)}, u32[]{:S(2)}, u32[]{:S(2)}) collective-permute-start(bf16[288,576]{1,0:T(8,128)(2,1)S(1)} %copy-done.26), channel_id=1, source_target_pairs={{0,1},{1,0},{2,3},{3,2},{4,5},{5,4},{6,7},{7,6},{8,9},{9,8},{10,11... | collective-permute-start | bytes 995336 | tf_op jit(solution)/shard_map/ppermute | solution.py:115
  12.2 27.1 %collective-permute-start.1 = (bf16[288,576]{1,0:T(8,128)(2,1)S(1)}, bf16[288,576]{1,0:T(8,128)(2,1)S(1)}, u32[]{:S(2)}, u32[]{:S(2)}) collective-permute-start(bf16[288,576]{1,0:T(8,128)(2,1)S(1)} %copy-done.26), channel_id=1, source_target_pairs={{0,2},{1,3},{2,0},{3,1},{4,6},{5,7},{6,4},{7,5},{8,10},{9,11},{10,... | collective-permute-start | bytes 995336 | tf_op jit(solution)/shard_map/ppermute | solution.py:115
  13.4 25.9 %collective-permute-start.2 = (bf16[288,576]{1,0:T(8,128)(2,1)S(1)}, bf16[288,576]{1,0:T(8,128)(2,1)S(1)}, u32[]{:S(2)}, u32[]{:S(2)}) collective-permute-start(bf16[288,576]{1,0:T(8,128)(2,1)S(1)} %copy-done.26), channel_id=1, source_target_pairs={{0,6},{1,7},{2,4},{3,5},{4,2},{5,3},{6,0},{7,1},{8,14},{9,15},{10,... | collective-permute-start | bytes 995336 | tf_op jit(solution)/shard_map/ppermute | solution.py:115
  15.2 25.7 %collective-permute-start.3 = (bf16[288,576]{1,0:T(8,128)(2,1)S(1)}, bf16[288,576]{1,0:T(8,128)(2,1)}, u32[]{:S(2)}, u32[]{:S(2)}) collective-permute-start(bf16[288,576]{1,0:T(8,128)(2,1)S(1)} %copy-done.26), channel_id=1, source_target_pairs={{0,4},{1,5},{2,6},{3,7},{4,0},{5,1},{6,2},{7,3},{8,12},{9,13},{10,... | collective-permute-start | bytes 995336 | tf_op jit(solution)/shard_map/ppermute | solution.py:115
  40.9 5.9 %collective-permute-start.4 = (bf16[8,288,384]{2,1,0:T(8,128)(2,1)S(1)}, bf16[8,288,384]{2,1,0:T(8,128)(2,1)S(1)}, u32[]{:S(2)}, u32[]{:S(2)}) collective-permute-start(bf16[8,288,384]{2,1,0:T(8,128)(2,1)S(1)} %all-to-all-done.own_ref), channel_id=1, source_target_pairs={{0,8},{8,0},{16,24},{24,16},{32,40},{40,32},{48,56},{56,48},{64,72... | collective-permute-start | bytes 5308424 | tf_op jit(solution)/shard_map/ppermute | solution.py:115
  43.2 23.3 %collective-permute-start.5 = (bf16[288,576]{1,0:T(8,128)(2,1)}, bf16[288,576]{1,0:T(8,128)(2,1)S(1)}, u32[]{:S(2)}, u32[]{:S(2)}) collective-permute-start(bf16[288,576]{1,0:T(8,128)(2,1)} %copy-done.27), channel_id=1, source_target_pairs={{0,2},{1,3},{2,0},{3,1},{4,6},{5,7},{6,4},{7,5},{8,10},{9,11},{10,... | collective-permute-start | bytes 995336 | tf_op jit(solution)/shard_map/ppermute | solution.py:115
  44.4 22.1 %collective-permute-start.6 = (bf16[288,576]{1,0:T(8,128)(2,1)}, bf16[288,576]{1,0:T(8,128)(2,1)S(1)}, u32[]{:S(2)}, u32[]{:S(2)}) collective-permute-start(bf16[288,576]{1,0:T(8,128)(2,1)} %copy-done.27), channel_id=1, source_target_pairs={{0,6},{1,7},{2,4},{3,5},{4,2},{5,3},{6,0},{7,1},{8,14},{9,15},{10,... | collective-permute-start | bytes 995336 | tf_op jit(solution)/shard_map/ppermute | solution.py:115
  46.2 20.3 %collective-permute-start.7 = (bf16[288,576]{1,0:T(8,128)(2,1)}, bf16[288,576]{1,0:T(8,128)(2,1)S(1)}, u32[]{:S(2)}, u32[]{:S(2)}) collective-permute-start(bf16[288,576]{1,0:T(8,128)(2,1)} %copy-done.27), channel_id=1, source_target_pairs={{0,4},{1,5},{2,6},{3,7},{4,0},{5,1},{6,2},{7,3},{8,12},{9,13},{10,... | collective-permute-start | bytes 995336 | tf_op jit(solution)/shard_map/ppermute | solution.py:115
  77.9 38.2 %all-to-all-start.1 = ((f32[128,16,128]{2,1,0:T(8,128)}), f32[128,16,128]{2,1,0:T(8,128)S(1)}, u32[]{:S(2)}, u32[]{:S(2)}) async-start(f32[128,16,128]{2,1,0:T(8,128)} %bitcast.61), calls=%async_computation.1 | async-start | bytes 2097152 | tf_op jit(solution)/shard_map/all_to_all | solution.py:294
  88.1 33.1 %collective-permute-start.11 = (f32[4,144,384]{2,1,0:T(8,128)}, f32[4,144,384]{2,1,0:T(8,128)S(1)}, u32[]{:S(2)}, u32[]{:S(2)}) collective-permute-start(f32[4,144,384]{2,1,0:T(8,128)} %get-tuple-element.104), channel_id=1, source_target_pairs={{0,1},{1,0},{2,3},{3,2},{4,5},{5,4},{6,7},{7,6},{8,9},{9,8},{10,11... | collective-permute-start | bytes 2654216 | tf_op jit(solution)/shard_map/ppermute | solution.py:115
  89.7 26.6 %collective-permute-start.10 = (f32[2,144,384]{2,1,0:T(8,128)}, f32[2,144,384]{2,1,0:T(8,128)S(1)}, u32[]{:S(2)}, u32[]{:S(2)}) collective-permute-start(f32[2,144,384]{2,1,0:T(8,128)} %get-tuple-element.102), channel_id=1, source_target_pairs={{0,4},{1,5},{2,6},{3,7},{4,0},{5,1},{6,2},{7,3},{8,12},{9,13},{10,... | collective-permute-start | bytes 1327112 | tf_op jit(solution)/shard_map/ppermute | solution.py:115
  92.4 27.4 %collective-permute-start.8 = (f32[2,144,384]{2,1,0:T(8,128)}, f32[2,144,384]{2,1,0:T(8,128)S(1)}, u32[]{:S(2)}, u32[]{:S(2)}) collective-permute-start(f32[2,144,384]{2,1,0:T(8,128)} %get-tuple-element.100), channel_id=1, source_target_pairs={{0,2},{1,3},{2,0},{3,1},{4,6},{5,7},{6,4},{7,5},{8,10},{9,11},{10,... | collective-permute-start | bytes 1327112 | tf_op jit(solution)/shard_map/ppermute | solution.py:115
  92.7 28.4 %collective-permute-start.9 = (f32[2,144,384]{2,1,0:T(8,128)}, f32[2,144,384]{2,1,0:T(8,128)S(1)}, u32[]{:S(2)}, u32[]{:S(2)}) collective-permute-start(f32[2,144,384]{2,1,0:T(8,128)} %get-tuple-element.101), channel_id=1, source_target_pairs={{0,6},{1,7},{2,4},{3,5},{4,2},{5,3},{6,0},{7,1},{8,14},{9,15},{10,... | collective-permute-start | bytes 1327112 | tf_op jit(solution)/shard_map/ppermute | solution.py:115
  121.1 30.6 %copy-start.8 = (f32[4,144,384]{2,1,0:T(8,128)}, f32[4,144,384]{2,1,0:T(8,128)S(1)}, u32[]{:S(2)}) copy-start(f32[4,144,384]{2,1,0:T(8,128)S(1)} %collective-permute-done.11) | copy-start | bytes 2654212
  121.1 10.3 %collective-permute-start.13 = (f32[8,144,576]{2,1,0:T(8,128)}, f32[8,144,576]{2,1,0:T(8,128)}, u32[]{:S(2)}, u32[]{:S(2)}) collective-permute-start(f32[8,144,576]{2,1,0:T(8,128)} %get-tuple-element.109), channel_id=1, source_target_pairs={{0,8},{8,0},{16,24},{24,16},{32,40},{40,32},{48,56},{56,48},{64,72... | collective-permute-start | bytes 7962632 | tf_op jit(solution)/shard_map/ppermute | solution.py:115
  122.1 14.4 %collective-permute-start.12 = (f32[8,144,576]{2,1,0:T(8,128)}, f32[8,144,576]{2,1,0:T(8,128)}, u32[]{:S(2)}, u32[]{:S(2)}) collective-permute-start(f32[8,144,576]{2,1,0:T(8,128)} %get-tuple-element.107), channel_id=1, source_target_pairs={{0,8},{8,0},{16,24},{24,16},{32,40},{40,32},{48,56},{56,48},{64,72... | collective-permute-start | bytes 7962632 | tf_op jit(solution)/shard_map/ppermute | solution.py:115
  123.3 26.4 %all-to-all-start.2 = ((f32[128,16,128]{2,1,0:T(8,128)}), f32[128,16,128]{2,1,0:T(8,128)S(1)}, u32[]{:S(2)}, u32[]{:S(2)}) async-start(f32[128,16,128]{2,1,0:T(8,128)} %broadcast_in_dim.7), calls=%async_computation.2 | async-start | bytes 2097152 | tf_op jit(solution)/shard_map/all_to_all | solution.py:299
  151.1 5.7 %collective-permute-start.18 = (f32[144,384]{1,0:T(8,128)S(1)}, f32[144,384]{1,0:T(8,128)S(1)}, u32[]{:S(2)}, u32[]{:S(2)}) collective-permute-start(f32[144,384]{1,0:T(8,128)S(1)} %add_bitcast_fusion.1), channel_id=1, source_target_pairs={{0,1},{1,0},{2,3},{3,2},{4,5},{5,4},{6,7},{7,6},{8,9},{9,8},{10,11... | collective-permute-start | bytes 663560 | tf_op jit(solution)/shard_map/ppermute | solution.py:115
  153.0 5.9 %collective-permute-start.19 = (f32[144,384]{1,0:T(8,128)S(1)}, f32[144,384]{1,0:T(8,128)S(1)}, u32[]{:S(2)}, u32[]{:S(2)}) collective-permute-start(f32[144,384]{1,0:T(8,128)S(1)} %get-tuple-element.171), channel_id=1, source_target_pairs={{0,2},{1,3},{2,0},{3,1},{4,6},{5,7},{6,4},{7,5},{8,10},{9,11},{10,... | collective-permute-start | bytes 663560 | tf_op jit(solution)/shard_map/ppermute | solution.py:115
  153.4 29.0 %copy-start.9 = (f32[144,384]{1,0:T(8,128)S(1)}, f32[144,384]{1,0:T(8,128)}, u32[]{:S(2)}) copy-start(f32[144,384]{1,0:T(8,128)} %get-tuple-element.132) | copy-start | bytes 663556
  153.4 22.3 %collective-permute-start.20 = (f32[144,384]{1,0:T(8,128)S(1)}, f32[144,384]{1,0:T(8,128)S(1)}, u32[]{:S(2)}, u32[]{:S(2)}) collective-permute-start(f32[144,384]{1,0:T(8,128)S(1)} %get-tuple-element.173), channel_id=1, source_target_pairs={{0,6},{1,7},{2,4},{3,5},{4,2},{5,3},{6,0},{7,1},{8,14},{9,15},{10,... | collective-permute-start | bytes 663560 | tf_op jit(solution)/shard_map/ppermute | solution.py:115
  155.3 34.1 %collective-permute-start.17 = (f32[4,144,576]{2,1,0:T(8,128)S(1)}, f32[4,144,576]{2,1,0:T(8,128)S(1)}, u32[]{:S(2)}, u32[]{:S(2)}) collective-permute-start(f32[4,144,576]{2,1,0:T(8,128)S(1)} %copy-done.4), channel_id=1, source_target_pairs={{0,64},{8,72},{16,80},{24,88},{32,96},{40,104},{48,112},{56,120},{... | collective-permute-start | bytes 3981320 | tf_op jit(solution)/shard_map/ppermute | solution.py:115
  156.5 26.9 %collective-permute-start.14 = (f32[2,144,576]{2,1,0:T(8,128)}, f32[2,144,576]{2,1,0:T(8,128)S(1)}, u32[]{:S(2)}, u32[]{:S(2)}) collective-permute-start(f32[2,144,576]{2,1,0:T(8,128)} %get-tuple-element.120), channel_id=1, source_target_pairs={{0,16},{8,24},{16,0},{24,8},{32,48},{40,56},{48,32},{56,40},{64,80... | collective-permute-start | bytes 1990664 | tf_op jit(solution)/shard_map/ppermute | solution.py:115
  156.9 26.5 %collective-permute-start.15 = (f32[2,144,576]{2,1,0:T(8,128)S(1)}, f32[2,144,576]{2,1,0:T(8,128)S(1)}, u32[]{:S(2)}, u32[]{:S(2)}) collective-permute-start(f32[2,144,576]{2,1,0:T(8,128)S(1)} %copy-done.17), channel_id=1, source_target_pairs={{0,48},{8,56},{16,32},{24,40},{32,16},{40,24},{48,0},{56,8},{64,11... | collective-permute-start | bytes 1990664 | tf_op jit(solution)/shard_map/ppermute | solution.py:115
  158.8 30.2 %collective-permute-start.16 = (f32[2,144,576]{2,1,0:T(8,128)S(1)}, f32[2,144,576]{2,1,0:T(8,128)S(1)}, u32[]{:S(2)}, u32[]{:S(2)}) collective-permute-start(f32[2,144,576]{2,1,0:T(8,128)S(1)} %copy-done.16), channel_id=1, source_target_pairs={{0,32},{8,40},{16,48},{24,56},{32,0},{40,8},{48,16},{56,24},{64,96... | collective-permute-start | bytes 1990664 | tf_op jit(solution)/shard_map/ppermute | solution.py:115
  175.7 6.7 %collective-permute-start.21 = (f32[144,384]{1,0:T(8,128)S(1)}, f32[144,384]{1,0:T(8,128)S(1)}, u32[]{:S(2)}, u32[]{:S(2)}) collective-permute-start(f32[144,384]{1,0:T(8,128)S(1)} %get-tuple-element.172), channel_id=1, source_target_pairs={{0,4},{1,5},{2,6},{3,7},{4,0},{5,1},{6,2},{7,3},{8,12},{9,13},{10,... | collective-permute-start | bytes 663560 | tf_op jit(solution)/shard_map/ppermute | solution.py:115
  191.9 37.1 %all-to-all-start.3 = ((bf16[8,288,384]{2,1,0:T(8,128)(2,1)}), bf16[8,288,384]{2,1,0:T(8,128)(2,1)}, u32[]{:S(2)}, u32[]{:S(2)}) async-start(bf16[8,288,384]{2,1,0:T(8,128)(2,1)} %broadcast_in_dim.8), calls=%async_computation.3 | async-start | bytes 3538944 | tf_op jit(solution)/shard_map/all_to_all | solution.py:388
  200.8 25.7 %collective-permute-start.22 = (f32[144,576]{1,0:T(8,128)S(1)}, f32[144,576]{1,0:T(8,128)S(1)}, u32[]{:S(2)}, u32[]{:S(2)}) collective-permute-start(f32[144,576]{1,0:T(8,128)S(1)} %add_bitcast_fusion), channel_id=1, source_target_pairs={{0,64},{8,72},{16,80},{24,88},{32,96},{40,104},{48,112},{56,120},{... | collective-permute-start | bytes 995336 | tf_op jit(solution)/shard_map/ppermute | solution.py:115
  201.4 25.3 %collective-permute-start.23 = (f32[144,576]{1,0:T(8,128)S(1)}, f32[144,576]{1,0:T(8,128)S(1)}, u32[]{:S(2)}, u32[]{:S(2)}) collective-permute-start(f32[144,576]{1,0:T(8,128)S(1)} %get-tuple-element.168), channel_id=1, source_target_pairs={{0,16},{8,24},{16,0},{24,8},{32,48},{40,56},{48,32},{56,40},{64,80... | collective-permute-start | bytes 995336 | tf_op jit(solution)/shard_map/ppermute | solution.py:115
  201.5 25.2 %collective-permute-start.24 = (f32[144,576]{1,0:T(8,128)S(1)}, f32[144,576]{1,0:T(8,128)S(1)}, u32[]{:S(2)}, u32[]{:S(2)}) collective-permute-start(f32[144,576]{1,0:T(8,128)S(1)} %get-tuple-element.170), channel_id=1, source_target_pairs={{0,48},{8,56},{16,32},{24,40},{32,16},{40,24},{48,0},{56,8},{64,11... | collective-permute-start | bytes 995336 | tf_op jit(solution)/shard_map/ppermute | solution.py:115
  202.4 24.2 %collective-permute-start.25 = (f32[144,576]{1,0:T(8,128)S(1)}, f32[144,576]{1,0:T(8,128)S(1)}, u32[]{:S(2)}, u32[]{:S(2)}) collective-permute-start(f32[144,576]{1,0:T(8,128)S(1)} %get-tuple-element.169), channel_id=1, source_target_pairs={{0,32},{8,40},{16,48},{24,56},{32,0},{40,8},{48,16},{56,24},{64,96... | collective-permute-start | bytes 995336 | tf_op jit(solution)/shard_map/ppermute | solution.py:115
  (31 other events, 293.7 us)
